TPU v7x, 32 devices: a whole 2x2x4 slice. The times are simulated.
32 devices in a mesh: orient: 16 (over z, y, core), coef: 2 (over x).
Axes of the slice: x: 2, y: 2, z: 4, core: 2. Of those that a mesh axis runs over, the one named last changes fastest.
Arguments:
- volume: bfloat16 [16, 12, 128, 128], P('orient', 'coef'), may hold values from -6 to 6
- measured: float32 [16, 16, 64, 128], P('orient'), may hold values from -6 to 6
- basis_table: float32 [16, 64, 12], P(None, None, 'coef'), may hold values from -1.75 to 1.75
- angle_table: float32 [16], replicated, may hold values from -1.2 to 1.2
- angle_index: int32 [16], P('orient'), may hold values from 0 to 15, each once
- sector_map: int32 [16, 64], P('orient'), may hold values from 0 to 63, each once within a row
Outputs:
- gradient: float32 [16, 12, 128, 128], P('orient', 'coef')
- residual: float32 [16, 16, 64, 128], P('orient', None, 'coef')
Inputs may be any that keep to these rules, and one draw needn't show every extreme that they name: `angle_index`: a permutation of the table orientations. `sector_map`: each row is a permutation of the 64 sectors.
All inputs are finite; a program needn't handle non-finite values.
Results may differ from a plain program's by a relative error of at most 0.02.
Values may be sent and summed in bfloat16 or wider, within the bound.
A program may use at most 64 MiB of HBM per device.

v0:
```python
import math

import jax
import jax.numpy as jnp
from jax import lax
from jax.sharding import PartitionSpec as P


def dft_tables(grid_size):
    midpoint = grid_size // 2
    row_ids = jnp.arange(grid_size, dtype=jnp.int32)
    frequency = jnp.where(row_ids <= midpoint, row_ids, row_ids - midpoint)
    positions = jnp.arange(grid_size, dtype=jnp.int32)
    products = frequency[:, None] * positions[None, :] % grid_size
    radians = products.astype(jnp.float32) * (2.0 * math.pi / grid_size)
    base_wave = jnp.where((row_ids > midpoint)[:, None], jnp.sin(radians), jnp.cos(radians))
    weights = jnp.where(
        (row_ids == 0) | (row_ids == midpoint), 1.0 / grid_size, 2.0 / grid_size
    ).astype(jnp.float32)
    return (base_wave.astype(jnp.bfloat16), (base_wave * weights[:, None]).astype(jnp.bfloat16))


def rotate(spectrum, shifts, axis_pos):
    length = spectrum.shape[axis_pos]
    midpoint = length // 2
    row_ids = jnp.arange(length, dtype=jnp.int32)
    frequency = jnp.where(row_ids <= midpoint, row_ids, row_ids - midpoint).astype(jnp.float32)
    sign_row = jnp.where(
        (row_ids > 0) & (row_ids < midpoint), -1.0, jnp.where(row_ids > midpoint, 1.0, 0.0)
    ).astype(jnp.float32)
    if axis_pos == -2:
        frequency = frequency[:, None]
        sign_row = sign_row[:, None]
    phases = shifts * frequency * (2.0 * math.pi / length)
    partner = jnp.roll(spectrum, midpoint, axis=axis_pos)
    return spectrum * jnp.cos(phases) + partner * (sign_row * jnp.sin(phases))


def shifts_for(angles, grid_size):
    positions = jnp.arange(grid_size, dtype=jnp.float32) - grid_size // 2
    slope_rows = -jnp.tan(angles * 0.5)
    slope_cols = jnp.sin(angles)
    row_shift = slope_rows[:, None, None, None] * positions[None, None, :, None]
    col_shift = slope_cols[:, None, None, None] * positions[None, None, None, :]
    return (row_shift, col_shift)


def forward_items(planes, angles, mixing, analysis, synthesis):
    grid_size = planes.shape[-1]
    row_shift, col_shift = shifts_for(angles, grid_size)
    wide = jnp.float32
    spectrum = jnp.einsum("kcyx,qx->kcyq", planes, analysis, preferred_element_type=wide)
    plane_field = jnp.einsum(
        "kcyq,qx->kcyx",
        rotate(spectrum, row_shift, -1).astype(jnp.bfloat16),
        synthesis,
        preferred_element_type=wide,
    ).astype(jnp.bfloat16)
    spectrum = jnp.einsum("qy,kcyx->kcqx", analysis, plane_field, preferred_element_type=wide)
    plane_field = jnp.einsum(
        "qn,kcqx->kcnx",
        synthesis,
        rotate(spectrum, col_shift, -2).astype(jnp.bfloat16),
        preferred_element_type=wide,
    ).astype(jnp.bfloat16)
    spectrum = jnp.einsum("kcyx,qx->kcyq", plane_field, analysis, preferred_element_type=wide)
    summed = jnp.sum(rotate(spectrum, row_shift, -1), axis=2).astype(jnp.bfloat16)
    profile = jnp.einsum("kcq,qx->kcx", summed, synthesis, preferred_element_type=wide) * (
        1.0 / math.sqrt(grid_size)
    )
    return jnp.einsum("ksc,kcx->ksx", mixing, profile, precision=lax.Precision.HIGHEST)


def backward_items(row_block, angles, analysis, synthesis):
    grid_size = row_block.shape[-1]
    row_shift, col_shift = shifts_for(angles, grid_size)
    wide = jnp.float32
    spectrum = jnp.einsum("kcx,qx->kcq", row_block, synthesis, preferred_element_type=wide)[
        :, :, None, :
    ]
    spread = (rotate(spectrum, -row_shift, -1) * (1.0 / math.sqrt(grid_size))).astype(jnp.bfloat16)
    plane_field = jnp.einsum("kcyq,qx->kcyx", spread, analysis, preferred_element_type=wide).astype(
        jnp.bfloat16
    )
    spectrum = jnp.einsum("qn,kcnx->kcqx", synthesis, plane_field, preferred_element_type=wide)
    plane_field = jnp.einsum(
        "qn,kcqx->kcnx",
        analysis,
        rotate(spectrum, -col_shift, -2).astype(jnp.bfloat16),
        preferred_element_type=wide,
    ).astype(jnp.bfloat16)
    spectrum = jnp.einsum("kcyx,qx->kcyq", plane_field, synthesis, preferred_element_type=wide)
    return jnp.einsum(
        "kcyq,qx->kcyx",
        rotate(spectrum, -row_shift, -1).astype(jnp.bfloat16),
        analysis,
        preferred_element_type=wide,
    )


def block_size(plane_count, orient_count):
    return plane_count * math.gcd(orient_count, max(1, 4 // plane_count))


def select_planes(planes, block_len):
    plane_count = planes.shape[0]
    return jnp.tile(planes, (block_len // plane_count, 1, 1, 1))


def project(planes, angles, mixing, analysis, synthesis):
    plane_count = planes.shape[0]
    orient_count = angles.shape[0]
    block_len = block_size(plane_count, orient_count)
    item_total = plane_count * orient_count

    def one_block(first_item):
        orient_ids = (first_item + jnp.arange(block_len, dtype=jnp.int32)) // plane_count
        chosen_planes = select_planes(planes, block_len)
        return forward_items(
            chosen_planes,
            jnp.take(angles, orient_ids),
            jnp.take(mixing, orient_ids, axis=0),
            analysis,
            synthesis,
        )

    starts = jnp.arange(item_total // block_len, dtype=jnp.int32) * block_len
    outputs = lax.map(one_block, starts)
    return outputs.reshape(orient_count, plane_count, outputs.shape[-2], outputs.shape[-1])


def backproject(contracted, angles, analysis, synthesis):
    orient_count, plane_count, coef_count, grid_size = contracted.shape
    block_len = block_size(plane_count, orient_count)
    item_total = plane_count * orient_count
    flat_rows = contracted.reshape(item_total, coef_count, grid_size)

    def add_block(accumulated, first_item):
        orient_ids = (first_item + jnp.arange(block_len, dtype=jnp.int32)) // plane_count
        row_block = lax.dynamic_slice_in_dim(flat_rows, first_item, block_len, 0)
        contrib = backward_items(row_block, jnp.take(angles, orient_ids), analysis, synthesis)
        accumulated = accumulated + contrib.reshape(
            block_len // plane_count, plane_count, coef_count, grid_size, grid_size
        ).sum(axis=0)
        return (accumulated, None)

    initial = jnp.zeros((plane_count, coef_count, grid_size, grid_size), jnp.float32)
    starts = jnp.arange(item_total // block_len, dtype=jnp.int32) * block_len
    return lax.scan(add_block, initial, starts)[0]


def geometry(indices, mapping, basis_table, angle_table):
    table_count = angle_table.shape[0]
    seg_count = mapping.shape[1]
    one_hot = (indices[:, None] == jnp.arange(table_count, dtype=jnp.int32)[None, :]).astype(
        jnp.float32
    )
    angles = jnp.dot(one_hot, angle_table, precision=lax.Precision.HIGHEST)
    chosen = jnp.einsum("oa,asc->osc", one_hot, basis_table, precision=lax.Precision.HIGHEST)
    permute = (mapping[:, :, None] == jnp.arange(seg_count, dtype=jnp.int32)[None, None, :]).astype(
        jnp.float32
    )
    mixing = jnp.einsum("ost,otc->osc", permute, chosen, precision=lax.Precision.HIGHEST)
    return (angles, mixing)


def body(volume, measured, basis_table, angle_table, angle_index, sector_map):
    grid_size = volume.shape[-1]
    analysis, synthesis = dft_tables(grid_size)
    seg_count = measured.shape[2]
    seg_share = seg_count // lax.axis_size("coef")
    all_index, all_map = (
        lax.all_gather(angle_index, "orient", axis=0, tiled=True),
        lax.all_gather(sector_map, "orient", axis=0, tiled=True),
    )
    angles, mixing = geometry(all_index, all_map, basis_table, angle_table)
    local_data = lax.all_to_all(
        measured.astype(jnp.bfloat16), "orient", split_axis=1, concat_axis=0, tiled=True
    ).astype(measured.dtype)
    signals = project(volume, angles, mixing, analysis, synthesis)
    signals = lax.psum(signals.astype(jnp.bfloat16), "coef").astype(jnp.float32)
    residual_full = signals - local_data
    start_seg = lax.axis_index("coef") * seg_share
    residual_share = lax.dynamic_slice_in_dim(residual_full, start_seg, seg_share, 2)
    contracted = jnp.einsum(
        "ozsx,osc->ozcx", residual_full, mixing, precision=lax.Precision.HIGHEST
    ).astype(jnp.bfloat16)
    gradient = backproject(contracted, angles, analysis, synthesis)
    residual = lax.all_to_all(
        residual_share.astype(jnp.bfloat16), "orient", split_axis=0, concat_axis=1, tiled=True
    ).astype(residual_share.dtype)
    return (gradient, residual)


def solution(mesh):
    placed = (
        P("orient", "coef", None, None),
        P("orient", None, None, None),
        P(None, None, "coef"),
        P(),
        P("orient"),
        P("orient", None),
    )
    return jax.shard_map(
        body,
        mesh=mesh,
        in_specs=placed,
        out_specs=(P("orient", "coef", None, None), P("orient", None, "coef", None)),
        check_vma=False,
    )
```

profile of v0, /device:TPU:0, one launch (start us, length us, event | category | flops | bytes accessed | tf_op | source)
XLA Modules:
  0.0 258.5 jit_solution(11013789148276880970)
XLA Ops:
  7.2 1.8 bitcast_convert_fusion
  9.0 7.4 %all-to-all-start = ((bf16[1,16,64,128]{3,2,0,1:T(8,128)(2,1)}), bf16[1,16,64,128]{3,2,0,1:T(8,128)(2,1)}, u32[]{:S(2)}, u32[]{:S(2)}) async-start(bf16[1,16,64,128]{3,2,0,1:T(8,128)(2,1)} %bitcast_convert_fusion), calls=%async_computation | async-start | bytes 524288 | tf_op jit(solution)/shard_map/all_to_all | solution.py:177
  19.7 12.3 %all-reduce = s32[16]{0:T(128)S(1)} all-reduce(s32[16]{0:T(128)S(1)} %dynamic-update-slice), channel_id=1, replica_groups=mesh['orient'=16,'coef'=2] {'orient'}, use_global_device_ids=true, to_apply=%add | all-reduce | flops 16 | bytes 128
  32.0 18.1 %all-gather = s32[16,1,64]{2,1,0:T(1,128)S(1)} all-gather(s32[1,1,64]{2,1,0:T(1,128)} %bitcast.155), channel_id=1, replica_groups=mesh['orient'=16,'coef'=2] {'orient'}, dimensions={0}, use_global_device_ids=true | all-gather | bytes 4352 | tf_op jit(solution)/shard_map/all_gather | solution.py:174
  51.7 91.9 %while.32 = (s32[]{:T(128)}, bf16[4,4,64,128]{3,2,1,0:T(8,128)(2,1)}, s32[4]{0:T(128)}, f32[16,64,6]{1,2,0:T(8,128)S(1)}, bf16[1,6,128,128]{3,2,1,0:T(8,128)(2,1...) while((s32[]{:T(128)}, ...), condition=%wide.region_2.4_spmd.clone.clone.clone, body=%wide.region_0.3_spmd.clone.clone.clone.sunk | while | flops 515168224 | bytes 30830560 | solution.py:128
  57.4 2.7 %fusion.244 = (f32[4,128,128]{1,2,0:T(8,128)S(1)}, f32[4,128,128]{1,2,0:T(8,128)}, f32[4,128,128]{1,2,0:T(8,128)S(1)}, f32[4,128,128]{1,2,0:T(8,128)S(1)}) fusion(f32[128]{0:T(128)S(1)} %fusion.242, f32[4,128]{1,0:T(4,128)S(1)} %get-tuple-element.652, f32[128]{0:T(128)S(1)} %and_select_fusion.6, f32[4,128]{1,0:T(4,128)S(1)} %get-tuple-element.653), kind=kLoop, calls=%fused_computation.35.clone.1 | loop fusion | flops 393216 | bytes 1053696 | tf_op jit(solution)/shard_map/while/body/eval_jaxpr/cos | solution.py:36
  61.8 1.6 fusion.240
  63.4 1.3 fusion.241
  64.7 2.7 %convolution_bitcast_fusion.6 = f32[4,6,128,128]{3,2,1,0:T(8,128)S(1)} fusion(f32[4,6,128,64]{2,3,1,0:T(8,128)} %get-tuple-element.648, f32[4,6,128,64]{2,3,1,0:T(8,128)} %get-tuple-element.649, f32[4,6,128,128]{2,3,1,0:T(8,128)S(1)} %fusion.240, f32[4,128,128]{1,2,0:T(8,128)} %get-tuple-element.654, f32[4,128,128]{1,2,0:T(8,128)S(1)} %get-tuple-element.655, ...), kind=kOutput, calls=%fused_computation.16.clone.1 | convolution fusion | flops 204226560 | bytes 5244032 | tf_op jit(solution)/shard_map/while/body/eval_jaxpr/qy,kcyx->kcqx/dot_general | solution.py:59
  67.4 1.3 fusion.245
  68.7 2.8 %fusion.246 = f32[4,6,128,128]{2,3,1,0:T(8,128)S(1)} fusion(f32[4,6,64,128]{3,2,1,0:T(8,128)} %get-tuple-element.656, f32[4,6,64,128]{3,2,1,0:T(8,128)} %get-tuple-element.657, f32[4,6,128,128]{3,2,1,0:T(8,128)S(1)} %convolution_bitcast_fusion.6, f32[4,128,128]{2,1,0:T(8,128)} %copy.51, f32[4,128,128]{2,1,0:T(8,128)} %copy.52, ...), kind=kOutput, calls=%fused_computation.20.clone.1 | convolution fusion | flops 204226560 | bytes 5244032 | tf_op jit(solution)/shard_map/while/body/eval_jaxpr/kcyx,qx->kcyq/dot_general | solution.py:66
  80.4 2.7 %fusion.244 = (f32[4,128,128]{1,2,0:T(8,128)S(1)}, f32[4,128,128]{1,2,0:T(8,128)}, f32[4,128,128]{1,2,0:T(8,128)S(1)}, f32[4,128,128]{1,2,0:T(8,128)S(1)}) fusion(f32[128]{0:T(128)S(1)} %fusion.242, f32[4,128]{1,0:T(4,128)S(1)} %get-tuple-element.652, f32[128]{0:T(128)S(1)} %and_select_fusion.6, f32[4,128]{1,0:T(4,128)S(1)} %get-tuple-element.653), kind=kLoop, calls=%fused_computation.35.clone.1 | loop fusion | flops 393216 | bytes 1053696 | tf_op jit(solution)/shard_map/while/body/eval_jaxpr/cos | solution.py:36
  84.8 1.6 fusion.240
  86.4 1.3 fusion.241
  87.7 2.7 %convolution_bitcast_fusion.6 = f32[4,6,128,128]{3,2,1,0:T(8,128)S(1)} fusion(f32[4,6,128,64]{2,3,1,0:T(8,128)} %get-tuple-element.648, f32[4,6,128,64]{2,3,1,0:T(8,128)} %get-tuple-element.649, f32[4,6,128,128]{2,3,1,0:T(8,128)S(1)} %fusion.240, f32[4,128,128]{1,2,0:T(8,128)} %get-tuple-element.654, f32[4,128,128]{1,2,0:T(8,128)S(1)} %get-tuple-element.655, ...), kind=kOutput, calls=%fused_computation.16.clone.1 | convolution fusion | flops 204226560 | bytes 5244032 | tf_op jit(solution)/shard_map/while/body/eval_jaxpr/qy,kcyx->kcqx/dot_general | solution.py:59
  90.4 1.3 fusion.245
  91.7 2.8 %fusion.246 = f32[4,6,128,128]{2,3,1,0:T(8,128)S(1)} fusion(f32[4,6,64,128]{3,2,1,0:T(8,128)} %get-tuple-element.656, f32[4,6,64,128]{3,2,1,0:T(8,128)} %get-tuple-element.657, f32[4,6,128,128]{3,2,1,0:T(8,128)S(1)} %convolution_bitcast_fusion.6, f32[4,128,128]{2,1,0:T(8,128)} %copy.51, f32[4,128,128]{2,1,0:T(8,128)} %copy.52, ...), kind=kOutput, calls=%fused_computation.20.clone.1 | convolution fusion | flops 204226560 | bytes 5244032 | tf_op jit(solution)/shard_map/while/body/eval_jaxpr/kcyx,qx->kcyq/dot_general | solution.py:66
  103.4 2.7 %fusion.244 = (f32[4,128,128]{1,2,0:T(8,128)S(1)}, f32[4,128,128]{1,2,0:T(8,128)}, f32[4,128,128]{1,2,0:T(8,128)S(1)}, f32[4,128,128]{1,2,0:T(8,128)S(1)}) fusion(f32[128]{0:T(128)S(1)} %fusion.242, f32[4,128]{1,0:T(4,128)S(1)} %get-tuple-element.652, f32[128]{0:T(128)S(1)} %and_select_fusion.6, f32[4,128]{1,0:T(4,128)S(1)} %get-tuple-element.653), kind=kLoop, calls=%fused_computation.35.clone.1 | loop fusion | flops 393216 | bytes 1053696 | tf_op jit(solution)/shard_map/while/body/eval_jaxpr/cos | solution.py:36
  107.8 1.6 fusion.240
  109.3 1.3 fusion.241
  110.6 2.7 %convolution_bitcast_fusion.6 = f32[4,6,128,128]{3,2,1,0:T(8,128)S(1)} fusion(f32[4,6,128,64]{2,3,1,0:T(8,128)} %get-tuple-element.648, f32[4,6,128,64]{2,3,1,0:T(8,128)} %get-tuple-element.649, f32[4,6,128,128]{2,3,1,0:T(8,128)S(1)} %fusion.240, f32[4,128,128]{1,2,0:T(8,128)} %get-tuple-element.654, f32[4,128,128]{1,2,0:T(8,128)S(1)} %get-tuple-element.655, ...), kind=kOutput, calls=%fused_computation.16.clone.1 | convolution fusion | flops 204226560 | bytes 5244032 | tf_op jit(solution)/shard_map/while/body/eval_jaxpr/qy,kcyx->kcqx/dot_general | solution.py:59
  114.6 2.8 %fusion.246 = f32[4,6,128,128]{2,3,1,0:T(8,128)S(1)} fusion(f32[4,6,64,128]{3,2,1,0:T(8,128)} %get-tuple-element.656, f32[4,6,64,128]{3,2,1,0:T(8,128)} %get-tuple-element.657, f32[4,6,128,128]{3,2,1,0:T(8,128)S(1)} %convolution_bitcast_fusion.6, f32[4,128,128]{2,1,0:T(8,128)} %copy.51, f32[4,128,128]{2,1,0:T(8,128)} %copy.52, ...), kind=kOutput, calls=%fused_computation.20.clone.1 | convolution fusion | flops 204226560 | bytes 5244032 | tf_op jit(solution)/shard_map/while/body/eval_jaxpr/kcyx,qx->kcyq/dot_general | solution.py:66
  126.3 2.7 %fusion.244 = (f32[4,128,128]{1,2,0:T(8,128)S(1)}, f32[4,128,128]{1,2,0:T(8,128)}, f32[4,128,128]{1,2,0:T(8,128)S(1)}, f32[4,128,128]{1,2,0:T(8,128)S(1)}) fusion(f32[128]{0:T(128)S(1)} %fusion.242, f32[4,128]{1,0:T(4,128)S(1)} %get-tuple-element.652, f32[128]{0:T(128)S(1)} %and_select_fusion.6, f32[4,128]{1,0:T(4,128)S(1)} %get-tuple-element.653), kind=kLoop, calls=%fused_computation.35.clone.1 | loop fusion | flops 393216 | bytes 1053696 | tf_op jit(solution)/shard_map/while/body/eval_jaxpr/cos | solution.py:36
  130.7 1.6 fusion.240
  132.3 1.3 fusion.241
  133.6 2.7 %convolution_bitcast_fusion.6 = f32[4,6,128,128]{3,2,1,0:T(8,128)S(1)} fusion(f32[4,6,128,64]{2,3,1,0:T(8,128)} %get-tuple-element.648, f32[4,6,128,64]{2,3,1,0:T(8,128)} %get-tuple-element.649, f32[4,6,128,128]{2,3,1,0:T(8,128)S(1)} %fusion.240, f32[4,128,128]{1,2,0:T(8,128)} %get-tuple-element.654, f32[4,128,128]{1,2,0:T(8,128)S(1)} %get-tuple-element.655, ...), kind=kOutput, calls=%fused_computation.16.clone.1 | convolution fusion | flops 204226560 | bytes 5244032 | tf_op jit(solution)/shard_map/while/body/eval_jaxpr/qy,kcyx->kcqx/dot_general | solution.py:59
  137.6 2.8 %fusion.246 = f32[4,6,128,128]{2,3,1,0:T(8,128)S(1)} fusion(f32[4,6,64,128]{3,2,1,0:T(8,128)} %get-tuple-element.656, f32[4,6,64,128]{3,2,1,0:T(8,128)} %get-tuple-element.657, f32[4,6,128,128]{3,2,1,0:T(8,128)S(1)} %convolution_bitcast_fusion.6, f32[4,128,128]{2,1,0:T(8,128)} %copy.51, f32[4,128,128]{2,1,0:T(8,128)} %copy.52, ...), kind=kOutput, calls=%fused_computation.20.clone.1 | convolution fusion | flops 204226560 | bytes 5244032 | tf_op jit(solution)/shard_map/while/body/eval_jaxpr/kcyx,qx->kcyq/dot_general | solution.py:66
  143.6 21.1 %all-reduce.3.cloned.1.call-done = bf16[16,1,64,128]{3,2,0,1:T(8,128)(2,1)} async-done(((bf16[16,1,64,128]{3,2,0,1:T(8,128)(2,1)}), bf16[16,1,64,128]{3,2,0,1:T(8,128)(2,1)}) %all-reduce.3.cloned.1.call-update) | async-done | bytes 262160 | tf_op jit(solution)/shard_map/psum | solution.py:181
  166.5 5.7 %all-to-all-start.1 = ((bf16[16,1,32,128]{3,2,1,0:T(8,128)(2,1)}), bf16[16,1,32,128]{3,2,1,0:T(8,128)(2,1)}, u32[]{:S(2)}, u32[]{:S(2)}) async-start(bf16[16,1,32,128]{3,2,1,0:T(8,128)(2,1)} %fusion.169), calls=%async_computation.1 | async-start | bytes 262144 | tf_op jit(solution)/shard_map/all_to_all | solution.py:189
  172.2 2.2 convolution_convert_fusion.4
  174.4 75.7 %while.33 = (s32[]{:T(128)}, f32[1,6,128,128]{3,2,1,0:T(8,128)}, s32[4]{0:T(128)}, bf16[16,6,128]{2,1,0:T(8,128)(2,1)}, f32[16]{0:T(128)S(1)}, /*index=5*/s32[12...) while((s32[]{:T(128)}, f32[1,6,128,128]{3,2,1,0:T(8,128)}, ...), condition=%wide.region_6.8_spmd.clone.clone.clone.clone, body=%wide.region_4.7_spmd.clone.clone.clone.clone.sunk | while | flops 513301952 | bytes 26328552 | solution.py:149
  181.0 3.0 %fusion.262 = (f32[4,128,128]{2,1,0:T(8,128)S(1)}, f32[4,128,128]{2,1,0:T(8,128)S(1)}, f32[4,128,128]{2,1,0:T(8,128)}, f32[4,128,128]{2,1,0:T(8,128)}) fusion(f32[128]{0:T(128)S(1)} %fusion.260, f32[4,128]{1,0:T(4,128)S(1)} %get-tuple-element.672, f32[128]{0:T(128)S(1)} %and_select_fusion.7, f32[4,128]{1,0:T(4,128)S(1)} %get-tuple-element.673), kind=kLoop, calls=%fused_computation.121.clone.1 | loop fusion | flops 393216 | bytes 1053696 | tf_op jit(solution)/shard_map/while/body/eval_jaxpr/cos | solution.py:36
  184.3 2.1 convolution_bitcast_fusion.7
  186.4 1.3 fusion.265
  187.7 2.8 %fusion.266 = f32[4,6,128,128]{2,3,1,0:T(8,128)S(1)} fusion(f32[4,6,64,128]{3,2,1,0:T(8,128)} %get-tuple-element.678, f32[4,6,64,128]{3,2,1,0:T(8,128)} %get-tuple-element.679, f32[4,6,128,128]{3,2,1,0:T(8,128)S(1)} %convolution_bitcast_fusion.7, f32[4,128,128]{2,1,0:T(8,128)} %get-tuple-element.680, f32[4,128,128]{2,1,0:T(8,128)} %get-tuple-element.681, ...), kind=kOutput, calls=%fused_computation.105.clone.1 | convolution fusion | flops 204226560 | bytes 5244032 | tf_op jit(solution)/shard_map/while/body/eval_jaxpr/kcyx,qx->kcyq/dot_general | solution.py:92
  200.0 3.0 %fusion.262 = (f32[4,128,128]{2,1,0:T(8,128)S(1)}, f32[4,128,128]{2,1,0:T(8,128)S(1)}, f32[4,128,128]{2,1,0:T(8,128)}, f32[4,128,128]{2,1,0:T(8,128)}) fusion(f32[128]{0:T(128)S(1)} %fusion.260, f32[4,128]{1,0:T(4,128)S(1)} %get-tuple-element.672, f32[128]{0:T(128)S(1)} %and_select_fusion.7, f32[4,128]{1,0:T(4,128)S(1)} %get-tuple-element.673), kind=kLoop, calls=%fused_computation.121.clone.1 | loop fusion | flops 393216 | bytes 1053696 | tf_op jit(solution)/shard_map/while/body/eval_jaxpr/cos | solution.py:36
  203.2 2.1 convolution_bitcast_fusion.7
  205.3 1.3 fusion.265
  206.6 2.8 %fusion.266 = f32[4,6,128,128]{2,3,1,0:T(8,128)S(1)} fusion(f32[4,6,64,128]{3,2,1,0:T(8,128)} %get-tuple-element.678, f32[4,6,64,128]{3,2,1,0:T(8,128)} %get-tuple-element.679, f32[4,6,128,128]{3,2,1,0:T(8,128)S(1)} %convolution_bitcast_fusion.7, f32[4,128,128]{2,1,0:T(8,128)} %get-tuple-element.680, f32[4,128,128]{2,1,0:T(8,128)} %get-tuple-element.681, ...), kind=kOutput, calls=%fused_computation.105.clone.1 | convolution fusion | flops 204226560 | bytes 5244032 | tf_op jit(solution)/shard_map/while/body/eval_jaxpr/kcyx,qx->kcyq/dot_general | solution.py:92
  218.9 3.0 %fusion.262 = (f32[4,128,128]{2,1,0:T(8,128)S(1)}, f32[4,128,128]{2,1,0:T(8,128)S(1)}, f32[4,128,128]{2,1,0:T(8,128)}, f32[4,128,128]{2,1,0:T(8,128)}) fusion(f32[128]{0:T(128)S(1)} %fusion.260, f32[4,128]{1,0:T(4,128)S(1)} %get-tuple-element.672, f32[128]{0:T(128)S(1)} %and_select_fusion.7, f32[4,128]{1,0:T(4,128)S(1)} %get-tuple-element.673), kind=kLoop, calls=%fused_computation.121.clone.1 | loop fusion | flops 393216 | bytes 1053696 | tf_op jit(solution)/shard_map/while/body/eval_jaxpr/cos | solution.py:36
  222.1 2.1 convolution_bitcast_fusion.7
  224.2 1.3 fusion.265
  225.5 2.8 %fusion.266 = f32[4,6,128,128]{2,3,1,0:T(8,128)S(1)} fusion(f32[4,6,64,128]{3,2,1,0:T(8,128)} %get-tuple-element.678, f32[4,6,64,128]{3,2,1,0:T(8,128)} %get-tuple-element.679, f32[4,6,128,128]{3,2,1,0:T(8,128)S(1)} %convolution_bitcast_fusion.7, f32[4,128,128]{2,1,0:T(8,128)} %get-tuple-element.680, f32[4,128,128]{2,1,0:T(8,128)} %get-tuple-element.681, ...), kind=kOutput, calls=%fused_computation.105.clone.1 | convolution fusion | flops 204226560 | bytes 5244032 | tf_op jit(solution)/shard_map/while/body/eval_jaxpr/kcyx,qx->kcyq/dot_general | solution.py:92
  237.8 3.0 %fusion.262 = (f32[4,128,128]{2,1,0:T(8,128)S(1)}, f32[4,128,128]{2,1,0:T(8,128)S(1)}, f32[4,128,128]{2,1,0:T(8,128)}, f32[4,128,128]{2,1,0:T(8,128)}) fusion(f32[128]{0:T(128)S(1)} %fusion.260, f32[4,128]{1,0:T(4,128)S(1)} %get-tuple-element.672, f32[128]{0:T(128)S(1)} %and_select_fusion.7, f32[4,128]{1,0:T(4,128)S(1)} %get-tuple-element.673), kind=kLoop, calls=%fused_computation.121.clone.1 | loop fusion | flops 393216 | bytes 1053696 | tf_op jit(solution)/shard_map/while/body/eval_jaxpr/cos | solution.py:36
  241.0 2.1 convolution_bitcast_fusion.7
  243.2 1.3 fusion.265
  244.4 2.8 %fusion.266 = f32[4,6,128,128]{2,3,1,0:T(8,128)S(1)} fusion(f32[4,6,64,128]{3,2,1,0:T(8,128)} %get-tuple-element.678, f32[4,6,64,128]{3,2,1,0:T(8,128)} %get-tuple-element.679, f32[4,6,128,128]{3,2,1,0:T(8,128)S(1)} %convolution_bitcast_fusion.7, f32[4,128,128]{2,1,0:T(8,128)} %get-tuple-element.680, f32[4,128,128]{2,1,0:T(8,128)} %get-tuple-element.681, ...), kind=kOutput, calls=%fused_computation.105.clone.1 | convolution fusion | flops 204226560 | bytes 5244032 | tf_op jit(solution)/shard_map/while/body/eval_jaxpr/kcyx,qx->kcyq/dot_general | solution.py:92
  250.1 1.6 bitcast_convert_fusion.1
  (234 shorter events, 81.4 us)
Async XLA Ops:
  7.2 43.7 %copy-start = (f32[16,64,6]{1,0,2:T(8,128)S(1)}, f32[16,64,6]{1,0,2:T(8,128)}, u32[]{:S(2)}) copy-start(f32[16,64,6]{1,0,2:T(8,128)} %param.14) | copy-start | bytes 73732
  9.0 155.7 %all-to-all-start = ((bf16[1,16,64,128]{3,2,0,1:T(8,128)(2,1)}), bf16[1,16,64,128]{3,2,0,1:T(8,128)(2,1)}, u32[]{:S(2)}, u32[]{:S(2)}) async-start(bf16[1,16,64,128]{3,2,0,1:T(8,128)(2,1)} %bitcast_convert_fusion), calls=%async_computation | async-start | bytes 524288 | tf_op jit(solution)/shard_map/all_to_all | solution.py:177
  16.4 148.3 %all-reduce.3.cloned.1.call-start = ((), (), s32[]{:S(2)}) async-start(), calls=%async_computation.2 | async-start | bytes 524288 | tf_op jit(solution)/shard_map/psum | solution.py:181
  71.5 1.0 copy-start.1
  72.4 1.0 copy-start.6
  72.4 1.0 copy-start.8
  74.0 0.7 copy-start.7
  94.5 1.0 copy-start.1
  95.4 1.0 copy-start.6
  95.4 1.0 copy-start.8
  97.0 0.7 copy-start.7
  117.4 1.0 copy-start.1
  118.4 1.0 copy-start.6
  118.4 1.0 copy-start.8
  119.9 0.7 copy-start.7
  140.4 1.0 copy-start.1
  141.3 1.0 copy-start.6
  141.3 1.0 copy-start.8
  142.9 0.7 copy-start.7
  166.5 83.5 %all-to-all-start.1 = ((bf16[16,1,32,128]{3,2,1,0:T(8,128)(2,1)}), bf16[16,1,32,128]{3,2,1,0:T(8,128)(2,1)}, u32[]{:S(2)}, u32[]{:S(2)}) async-start(bf16[16,1,32,128]{3,2,1,0:T(8,128)(2,1)} %fusion.169), calls=%async_computation.1 | async-start | bytes 262144 | tf_op jit(solution)/shard_map/all_to_all | solution.py:189
  184.3 3.4 %copy-start.2 = (f32[4,128,128]{1,2,0:T(8,128)}, f32[4,128,128]{1,2,0:T(8,128)S(1)}, u32[]{:S(2)}) copy-start(f32[4,128,128]{1,2,0:T(8,128)S(1)} %copy.54) | copy-start | bytes 786436 | tf_op jit(solution)/shard_map/while
  190.5 1.0 copy-start.3
  191.5 1.0 copy-start.4
  192.6 0.7 copy-start.5
  203.2 3.4 %copy-start.2 = (f32[4,128,128]{1,2,0:T(8,128)}, f32[4,128,128]{1,2,0:T(8,128)S(1)}, u32[]{:S(2)}) copy-start(f32[4,128,128]{1,2,0:T(8,128)S(1)} %copy.54) | copy-start | bytes 786436 | tf_op jit(solution)/shard_map/while
  209.4 1.0 copy-start.3
  210.4 1.0 copy-start.4
  211.5 0.7 copy-start.5
  222.1 3.4 %copy-start.2 = (f32[4,128,128]{1,2,0:T(8,128)}, f32[4,128,128]{1,2,0:T(8,128)S(1)}, u32[]{:S(2)}) copy-start(f32[4,128,128]{1,2,0:T(8,128)S(1)} %copy.54) | copy-start | bytes 786436 | tf_op jit(solution)/shard_map/while
  228.3 1.0 copy-start.3
  229.3 1.0 copy-start.4
  230.4 0.7 copy-start.5
  241.0 3.4 %copy-start.2 = (f32[4,128,128]{1,2,0:T(8,128)}, f32[4,128,128]{1,2,0:T(8,128)S(1)}, u32[]{:S(2)}) copy-start(f32[4,128,128]{1,2,0:T(8,128)S(1)} %copy.54) | copy-start | bytes 786436 | tf_op jit(solution)/shard_map/while
  247.2 1.0 copy-start.3
  248.2 1.0 copy-start.4
  249.3 0.7 copy-start.5
Sparse Core Ops, SparseCore 0:
  143.7 20.9 all-reduce.2
where the time goes:
time: 260 us; the launch traced here: 259 us
  matrix products  63.7 us (24%)
  local copies, waits for them, and re-layouts  56.9 us (22%)
  other arithmetic  49.8 us (19%)
  blocking collectives  30.3 us (12%)
  waiting for transfers between devices  21.1 us (8%)
  between operations  14.8 us (6%)
  starting transfers between devices  13.2 us (5%)
  loops' own time  8.64 us (3%)
    cos x8, other arithmetic, rotate(): return spectrum * jnp.cos(phases) + partner * (sign_row * jnp.sin(phases))  22.7 us
    psum x1, waiting for transfers between devices, body(): signals = lax.psum(signals.astype(jnp.bfloat16), 'coef').astype(jnp.float32)  21.1 us
    all_gather x1, blocking collectives, body(): lax.all_gather(sector_map, 'orient', axis=0, tiled=True)  18.1 us
    slice x24, local copies, waits for them, and re-layouts, rotate(): partner = jnp.roll(spectrum, midpoint, axis=axis_pos)  16.7 us
    while x64, local copies, waits for them, and re-layouts  12.9 us
    unnamed x1, blocking collectives  12.3 us
    dot_general x4, matrix products, backward_items(): jnp.einsum('kcyx,qx->kcyq', plane_field, synthesis, preferred_element_typ...  11.2 us
    dot_general x4, matrix products, forward_items(): jnp.einsum('kcyx,qx->kcyq', plane_field, analysis, preferred_element_type...  11.2 us
  transfers between devices with their start and end apart: 3, of which 1 were waited for; matrix products, arithmetic and copies ran while one was open for 59% of the time, Pallas kernels for 0%

commit v1 on v0

v1 whole, which is shorter than its diff:
```python
import functools
import math

import jax
import jax.numpy as jnp
from jax import lax
from jax.experimental import pallas as pl
from jax.experimental.pallas import tpu as pltpu
from jax.sharding import PartitionSpec as P

WIDE = jnp.float32
NARROW = jnp.bfloat16


def dft_tables(grid_size):
    midpoint = grid_size // 2
    row_ids = jnp.arange(grid_size, dtype=jnp.int32)
    frequency = jnp.where(row_ids <= midpoint, row_ids, row_ids - midpoint)
    positions = jnp.arange(grid_size, dtype=jnp.int32)
    products = frequency[:, None] * positions[None, :] % grid_size
    radians = products.astype(jnp.float32) * (2.0 * math.pi / grid_size)
    base_wave = jnp.where((row_ids > midpoint)[:, None], jnp.sin(radians), jnp.cos(radians))
    weights = jnp.where(
        (row_ids == 0) | (row_ids == midpoint), 1.0 / grid_size, 2.0 / grid_size
    ).astype(jnp.float32)
    return (base_wave.astype(jnp.bfloat16), (base_wave * weights[:, None]).astype(jnp.bfloat16))


def cmul(left, right):
    return (
        left[0] * right[0] - left[1] * right[1],
        left[0] * right[1] + left[1] * right[0],
    )


def power_rows(base, bits, rows, lanes):
    ids = lax.broadcasted_iota(jnp.int32, (rows, lanes), 0)
    result = None
    for bit in range(bits):
        on = (ids // (1 << bit)) % 2 == 1
        term = (jnp.where(on, base[0], 1.0), jnp.where(on, base[1], 0.0))
        result = term if result is None else cmul(result, term)
        base = cmul(base, base)
    return result, base


def unit_waves(angles, grid_size, unit_ref):
    half = grid_size // 2
    count = angles.shape[0]
    lanes = lax.broadcasted_iota(jnp.int32, (count, grid_size), 1)
    frequency = jnp.where(lanes <= half, lanes, lanes - half).astype(WIDE)
    unit = 2.0 * math.pi / grid_size
    slope_rows = -jnp.sin(angles * 0.5) / jnp.cos(angles * 0.5)
    row_phase = slope_rows * frequency * unit
    col_phase = jnp.sin(angles) * (lanes - half).astype(WIDE) * unit
    unit_ref[0] = jnp.cos(row_phase)
    unit_ref[1] = jnp.sin(row_phase)
    unit_ref[2] = jnp.cos(col_phase)
    unit_ref[3] = jnp.sin(col_phase)


def build_tables(which, grid_size, unit_ref, row_ref, col_ref, mix_ref, slot, synthesis):
    half = grid_size // 2
    lanes = lax.broadcasted_iota(jnp.int32, (8, grid_size), 1)
    sign = jnp.where(lanes > half, 1.0, jnp.where((lanes > 0) & (lanes < half), -1.0, 0.0))
    coarse_count = grid_size // 8
    bits = coarse_count.bit_length() - 1

    def take(at):
        return unit_ref[at, pl.ds(which, 1), :]

    fine, eighth = power_rows((take(0), take(1)), 3, 8, grid_size)
    coarse, top = power_rows(eighth, bits, coarse_count, grid_size)
    middle = (coarse[0][half // 8 : half // 8 + 1], coarse[1][half // 8 : half // 8 + 1])
    coarse = cmul(coarse, (middle[0], -middle[1]))
    for j in range(coarse_count):
        wave = cmul((coarse[0][j : j + 1], coarse[1][j : j + 1]), fine)
        row_ref[slot, 0, 8 * j : 8 * j + 8, :] = wave[0]
        row_ref[slot, 1, 8 * j : 8 * j + 8, :] = wave[1] * sign
    for part in range(2):
        mix_ref[slot, part] = jnp.dot(
            synthesis, row_ref[slot, part].astype(NARROW), preferred_element_type=WIDE
        )
    fine, eighth = power_rows((take(2), take(3)), 3, 8, grid_size)
    coarse, highest = power_rows(eighth, bits - 1, coarse_count // 2, grid_size)
    first = lax.broadcasted_iota(jnp.int32, (8, grid_size), 0) == 0
    for j in range(coarse_count // 2):
        wave = cmul((coarse[0][j : j + 1], coarse[1][j : j + 1]), fine)
        col_ref[slot, 0, 8 * j : 8 * j + 8, :] = wave[0]
        col_ref[slot, 1, 8 * j : 8 * j + 8, :] = -wave[1]
        low = wave[0] if j else jnp.where(first, highest[0], wave[0])
        col_ref[slot, 0, half + 8 * j : half + 8 * j + 8, :] = low
        col_ref[slot, 1, half + 8 * j : half + 8 * j + 8, :] = wave[1]


def swap_rows(field):
    half = field.shape[0] // 2
    return jnp.concatenate([field[half:], field[:half]], axis=0)


def mul(left, right):
    return jnp.dot(left, right, preferred_element_type=WIDE)


def image_groups(count, width=2):
    return [range(at, min(at + width, count)) for at in range(0, count, width)]


def volume_spectra(volume_ref, analysis_t, spec_ref, images, grid_size):
    for image in range(images):
        spectrum = mul(volume_ref[image], analysis_t)
        spec_ref[0, image] = spectrum
        spec_ref[1, image] = pltpu.roll(spectrum, grid_size // 2, 1)


def forward_one(slot, images, grid_size, spec_ref, row_ref, col_ref, mix_ref, waves):
    analysis, analysis_t, synthesis = waves
    sums, rolled = [], []
    for group in image_groups(images):
        fields = []
        for image in group:
            turned = spec_ref[0, image] * row_ref[slot, 0] + spec_ref[1, image] * row_ref[slot, 1]
            fields.append(mul(turned.astype(NARROW), synthesis).astype(NARROW))
        spectrum = mul(analysis, jnp.concatenate(fields, axis=1))
        for at in range(len(group)):
            own = spectrum[:, at * grid_size : (at + 1) * grid_size]
            turned = own * col_ref[slot, 0] + swap_rows(own) * col_ref[slot, 1]
            last = mul(turned.astype(NARROW), analysis_t)
            sums.append(jnp.sum(last * mix_ref[slot, 0], axis=0, keepdims=True))
            rolled.append(jnp.sum(last * mix_ref[slot, 1], axis=0, keepdims=True))
    total = jnp.concatenate(sums, axis=0)
    crossed = pltpu.roll(jnp.concatenate(rolled, axis=0), grid_size // 2, 1)
    summed = (total - crossed).astype(NARROW)
    return mul(summed, synthesis) * (1.0 / math.sqrt(grid_size))


def backward_one(slot, rows, grid_size, total_ref, row_ref, col_ref, mix_ref, waves):
    analysis, analysis_t, synthesis_t = waves
    images = rows.shape[0]
    spectra = mul(rows, synthesis_t) * (1.0 / math.sqrt(grid_size))
    crossed = pltpu.roll(spectra, grid_size // 2, 1)
    for group in image_groups(images):
        fields = []
        for image in group:
            spread = (
                spectra[image : image + 1] * mix_ref[slot, 0]
                - crossed[image : image + 1] * mix_ref[slot, 1]
            )
            own = mul(spread.astype(NARROW), analysis)
            turned = own * col_ref[slot, 0] - swap_rows(own) * col_ref[slot, 1]
            fields.append(turned.astype(NARROW))
        field = mul(analysis_t, jnp.concatenate(fields, axis=1)).astype(NARROW)
        for at, image in enumerate(group):
            own = mul(field[:, at * grid_size : (at + 1) * grid_size], synthesis_t)
            total_ref[image] += (
                own * row_ref[slot, 0]
                - pltpu.roll(own, grid_size // 2, 1) * row_ref[slot, 1]
            )


def forward_kernel(
    volume_ref, angle_ref, ana_ref, ana_t_ref, syn_ref, out_ref, unit_ref, spec_ref, row_ref, col_ref, mix_ref
):
    images, grid_size = volume_ref.shape[0], volume_ref.shape[-1]
    unit_waves(angle_ref[...], grid_size, unit_ref)
    volume_spectra(volume_ref, ana_t_ref[...], spec_ref, images, grid_size)

    def step(which, carry):
        build_tables(which, grid_size, unit_ref, row_ref, col_ref, mix_ref, 0, syn_ref[...])
        waves = (ana_ref[...], ana_t_ref[...], syn_ref[...])
        out_ref[which] = forward_one(0, images, grid_size, spec_ref, row_ref, col_ref, mix_ref, waves)
        return carry

    lax.fori_loop(0, out_ref.shape[0], step, 0)


def backward_kernel(
    rows_ref, angle_ref, ana_ref, ana_t_ref, syn_ref, syn_t_ref, out_ref, unit_ref, total_ref, row_ref, col_ref, mix_ref
):
    images, grid_size = out_ref.shape[0], out_ref.shape[-1]
    unit_waves(angle_ref[...], grid_size, unit_ref)
    total_ref[...] = jnp.zeros_like(total_ref)

    def step(which, carry):
        build_tables(which, grid_size, unit_ref, row_ref, col_ref, mix_ref, 0, syn_ref[...])
        waves = (ana_ref[...], ana_t_ref[...], syn_t_ref[...])
        backward_one(
            0, rows_ref[which].astype(NARROW), grid_size, total_ref, row_ref, col_ref, mix_ref, waves
        )
        return carry

    lax.fori_loop(0, rows_ref.shape[0], step, 0)
    for image in range(images):
        out_ref[image] = mul(total_ref[image].astype(NARROW), ana_ref[...])


VMEM = functools.partial(pl.BlockSpec, memory_space=pltpu.VMEM)
LIMIT = 40 << 20


def table_scratch(count, grid_size, slots):
    return [
        pltpu.VMEM((4, count, grid_size), WIDE),
        pltpu.VMEM((slots, 2, grid_size, grid_size), WIDE),
        pltpu.VMEM((slots, 2, grid_size, grid_size), WIDE),
        pltpu.VMEM((slots, 2, grid_size, grid_size), WIDE),
    ]


def exact(pattern, left, right):
    return jnp.einsum(pattern, left, right, precision=lax.Precision.HIGHEST)


def body(volume, measured, basis_table, angle_table, angle_index, sector_map):
    grid_size = volume.shape[-1]
    images = volume.shape[0] * volume.shape[1]
    own_coefs = basis_table.shape[2]
    table_count = angle_table.shape[0]
    seg_count = measured.shape[2]
    seg_share = seg_count // lax.axis_size("coef")
    analysis, synthesis = dft_tables(grid_size)
    angles = jnp.broadcast_to(angle_table[:, None], (table_count, grid_size))
    unit_s, row_s, col_s, mix_s = table_scratch(table_count, grid_size, 1)

    table_ids = jnp.arange(table_count, dtype=jnp.int32)
    own_hot = (angle_index[0] == table_ids).astype(WIDE)
    permute = (sector_map[0][:, None] == jnp.arange(seg_count, dtype=jnp.int32)).astype(WIDE)
    own_mix = exact("st,tc->sc", permute, exact("a,asc->sc", own_hot, basis_table))
    pulled = exact("zsx,sc->zcx", measured[0], own_mix)
    tagged = jnp.concatenate(
        [pulled, jnp.broadcast_to(angle_index[0].astype(WIDE), (pulled.shape[0], 1, grid_size))],
        axis=1,
    )
    arrived = lax.all_to_all(tagged, "orient", split_axis=0, concat_axis=0, tiled=True)
    basis_full = lax.all_gather(basis_table, "coef", axis=2, tiled=True)

    profiles = pl.pallas_call(
        forward_kernel,
        out_shape=jax.ShapeDtypeStruct((table_count, images, grid_size), WIDE),
        in_specs=[VMEM()] * 5,
        out_specs=VMEM(),
        scratch_shapes=[unit_s, pltpu.VMEM((2, images, grid_size, grid_size), WIDE), row_s, col_s, mix_s],
        compiler_params=pltpu.CompilerParams(vmem_limit_bytes=LIMIT),
    )(volume.reshape(images, grid_size, grid_size), angles, analysis, analysis.T, synthesis)

    all_profiles = lax.all_gather(profiles, "coef", axis=1, tiled=True)
    hot = (arrived[:, own_coefs, 0].astype(jnp.int32)[:, None] == table_ids).astype(WIDE)
    gram = exact("asc,asd->acd", basis_table, basis_full)
    contracted = exact("acd,adx->acx", gram, all_profiles) - exact(
        "oa,ocx->acx", hot, arrived[:, :own_coefs]
    )
    gradient = pl.pallas_call(
        backward_kernel,
        out_shape=jax.ShapeDtypeStruct((images, grid_size, grid_size), WIDE),
        in_specs=[VMEM()] * 6,
        out_specs=VMEM(),
        scratch_shapes=[unit_s, pltpu.VMEM((images, grid_size, grid_size), WIDE), row_s, col_s, mix_s],
        compiler_params=pltpu.CompilerParams(vmem_limit_bytes=LIMIT),
    )(contracted, angles, analysis, analysis.T, synthesis, synthesis.T)

    returned = lax.all_to_all(
        exact("oa,acx->ocx", hot, all_profiles), "orient", split_axis=0, concat_axis=0, tiled=True
    )
    full_mix = exact("st,tc->sc", permute, exact("a,asc->sc", own_hot, basis_full))
    start_seg = lax.axis_index("coef") * seg_share
    share_mix = lax.dynamic_slice_in_dim(full_mix, start_seg, seg_share, 0)
    share_data = lax.dynamic_slice_in_dim(measured[0], start_seg, seg_share, 1)
    residual = exact("sc,zcx->zsx", share_mix, returned) - share_data
    return (gradient.reshape(volume.shape), residual[None])


def solution(mesh):
    placed = (
        P("orient", "coef", None, None),
        P("orient", None, None, None),
        P(None, None, "coef"),
        P(),
        P("orient"),
        P("orient", None),
    )
    return jax.shard_map(
        body,
        mesh=mesh,
        in_specs=placed,
        out_specs=(P("orient", "coef", None, None), P("orient", None, "coef", None)),
        check_vma=False,
    )
```

time: 260 us -> 78.9 us (0.30)
  matrix products: 63.7 us -> 5.24 us
  local copies, waits for them, and re-layouts: 56.9 us -> 2.95 us
  other arithmetic: 49.8 us -> 1.01 us
  Pallas kernels: 0 us -> 44.8 us
  waiting for transfers between devices: 21.1 us -> 0.01 us
  blocking collectives: 30.3 us -> 9.53 us
  between operations: 14.8 us -> 1.4 us
  loops' own time: 8.64 us -> 0 us
    dot_general x40 -> x10, matrix products: 63.7 us -> 5.24 us  [exact(): return jnp.einsum(pattern, left, right, precision=lax.Precision.HIGHEST)]
    pallas_call x0 -> x2, Pallas kernels: none -> 44.8 us  [the longest x1 23.3 us: body(): pl.pallas_call(backward_kernel, out_shape=jax.ShapeDtypeStruct((images, g...]
    cos x8 -> x0, other arithmetic: 22.7 us -> none  [rotate(): return spectrum * jnp.cos(phases) + partner * (sign_row * jnp.sin(phases))]
    psum x1 -> x0, waiting for transfers between devices: 21.1 us -> none  [body(): signals = lax.psum(signals.astype(jnp.bfloat16), 'coef').astype(jnp.float32)]
    slice x24 -> x0, local copies, waits for them, and re-layouts: 16.7 us -> none  [rotate(): partner = jnp.roll(spectrum, midpoint, axis=axis_pos)]
    while x64 -> x0, local copies, waits for them, and re-layouts: 12.9 us -> none
    unnamed x1 -> x0, blocking collectives: 12.3 us -> none
    dynamic_slice x8 -> x0, local copies, waits for them, and re-layouts: 9.6 us -> none  [project(): outputs = lax.map(one_block, starts)]
  transfers between devices with their start and end apart: 3 -> 2, of which waited for: 1 -> 0; matrix products, arithmetic and copies ran while one was open for 59% -> 2% of each run, Pallas kernels for 0% -> 57%
where the time goes in v1:
time: 78.9 us; the launch traced here: 78.4 us
  Pallas kernels  44.8 us (57%)
  starting transfers between devices  13.5 us (17%)
  blocking collectives  9.53 us (12%)
  matrix products  5.24 us (7%)
  local copies, waits for them, and re-layouts  2.95 us (4%)
  between operations  1.4 us (2%)
  other arithmetic  1.01 us (1%)
    pallas_call x1, Pallas kernels, body(): pl.pallas_call(backward_kernel, out_shape=jax.ShapeDtypeStruct((images, g...  23.3 us
    pallas_call x1, Pallas kernels, body(): pl.pallas_call(forward_kernel, out_shape=jax.ShapeDtypeStruct((table_coun...  21.5 us
    all_to_all x1, starting transfers between devices, body(): lax.all_to_all(tagged, 'orient', split_axis=0, concat_axis=0, tiled=True)  7.52 us
    all_to_all x1, starting transfers between devices, body(): lax.all_to_all(exact('oa,acx->ocx', hot, all_profiles), 'orient', split_a...  6.01 us
    dot_general x10, matrix products, exact(): return jnp.einsum(pattern, left, right, precision=lax.Precision.HIGHEST)  5.24 us
    all_gather x1, blocking collectives, body(): basis_full = lax.all_gather(basis_table, 'coef', axis=2, tiled=True)  4.77 us
    all_gather x1, blocking collectives, body(): all_profiles = lax.all_gather(profiles, 'coef', axis=1, tiled=True)  4.77 us
  transfers between devices with their start and end apart: 2, of which 0 were waited for; matrix products, arithmetic and copies ran while one was open for 2% of the time, Pallas kernels for 57%

profile of v1, /device:TPU:0, one launch (start us, length us, event | category | flops | bytes accessed | tf_op | source)
XLA Modules:
  0.0 78.4 jit_solution(16382591581684465052)
XLA Ops:
  1.3 0.9 %fusion.39 = f32[1,64,6]{1,0,2:T(1,128)S(1)} fusion(f32[16,64,6]{1,0,2:T(8,128)} %param.8, s32[]{:T(128)} %bitcast.48), kind=kOutput, calls=%fused_computation.55 | convolution fusion | flops 73744 | bytes 26116 | tf_op jit(solution)/shard_map/a,asc->sc/dot_general | solution.py:211
  2.2 0.1 copy.28
  2.3 0.0 copy-start.4
  2.3 0.7 copy-done.4
  3.0 0.2 convolution_bitcast_fusion.2
  3.2 1.4 %convolution_bitcast_fusion.1 = f32[16,6,128]{2,1,0:T(8,128)S(1)} fusion(f32[64,6,1]{0,1,2:T(8,128)S(1)} %convolution_bitcast_fusion.2, f32[1,16,64,128]{3,2,1,0:T(8,128)} %param.7), kind=kOutput, calls=%fused_computation.4 | convolution fusion | flops 9437184 | bytes 574976 | tf_op jit(solution)/shard_map/zsx,sc->zcx/dot_general | solution.py:211
  4.6 0.6 concatenate.3
  5.2 0.0 copy-start.2
  5.2 7.5 %all-to-all-start = ((f32[16,7,128]{2,1,0:T(8,128)}), f32[16,7,128]{2,1,0:T(8,128)S(1)}, u32[]{:S(2)}, u32[]{:S(2)}) async-start(f32[16,7,128]{2,1,0:T(8,128)} %concatenate.3), calls=%async_computation | async-start | bytes 131072 | tf_op jit(solution)/shard_map/all_to_all | solution.py:234
  12.8 0.0 copy-done.2
  12.8 4.8 %all_gather.6 = f32[16,64,12]{1,0,2:T(8,128)S(1)} all-gather(f32[16,64,6]{1,0,2:T(8,128)S(1)} %copy-done.2), channel_id=1, replica_groups=mesh['orient'=16,'coef'=2] {'coef'}, dimensions={2}, use_global_device_ids=true | all-gather | bytes 73728 | tf_op jit(solution)/shard_map/all_gather | solution.py:235
  17.6 0.3 fusion.4
  17.9 0.0 copy-start
  17.9 0.2 fusion.37
  18.1 0.1 copy.30
  18.2 0.6 multiply_convert_fusion
  18.8 0.2 fusion.21
  19.0 0.0 copy-start.3
  19.0 0.7 copy-done.3
  19.7 0.1 broadcast_in_dim.45.angle_ref
  19.8 0.0 copy-done
  19.8 21.5 %shard_map.77 = f32[16,6,128]{2,1,0:T(8,128)S(1)} custom-call(bf16[6,128,128]{2,1,0:T(8,128)(2,1)S(1)} %bitcast.51, f32[16,128]{1,0:T(8,128)S(1)} %broadcast_in_dim.45.angle_ref, bf16[128,128]{1,0:T(8,128)(2,1)S(1)} %get-tuple-element.5.ana_ref, bf16[128,128]{1,0:T(8,128)(2,1)S(1)} %get-tuple-element.4.ana_t_ref, bf16[128,128]{1,0:T(8,128)(2,1)S(1)} %get-tuple-element.3.syn_ref), custom_call_target="tpu_custom_call" | custom-call | tf_op jit(solution)/shard_map/pallas_call | solution.py:237
  41.3 4.8 %all_gather.7 = f32[16,12,128]{2,0,1:T(8,128)S(1)} all-gather(f32[16,6,128]{2,0,1:T(8,128)S(1)} %copy.22), channel_id=1, replica_groups=mesh['orient'=16,'coef'=2] {'coef'}, dimensions={1}, use_global_device_ids=true | all-gather | bytes 147456 | tf_op jit(solution)/shard_map/all_gather | solution.py:246
  46.0 0.0 all-to-all-done
  46.0 0.4 fusion.28
  46.4 0.3 fusion.19
  46.7 0.2 fusion.32
  47.0 0.7 copy.27
  47.7 6.0 %all-to-all-start.1 = ((f32[16,12,128]{2,1,0:T(8,128)}), f32[16,12,128]{2,1,0:T(8,128)S(1)}, u32[]{:S(2)}, u32[]{:S(2)}) async-start(f32[16,12,128]{2,1,0:T(8,128)} %copy.27), calls=%async_computation.1 | async-start | bytes 262144 | tf_op jit(solution)/shard_map/all_to_all | solution.py:261
  53.7 0.0 copy-start.1
  53.7 0.3 convolution_subtract_fusion.rows_ref
  53.9 23.3 %shard_map.78 = f32[6,128,128]{2,1,0:T(8,128)} custom-call(f32[16,6,128]{2,1,0:T(8,128)S(1)} %convolution_subtract_fusion.rows_ref, f32[16,128]{1,0:T(8,128)S(1)} %broadcast_in_dim.45.angle_ref, bf16[128,128]{1,0:T(8,128)(2,1)S(1)} %get-tuple-element.5.ana_ref, bf16[128,128]{1,0:T(8,128)(2,1)S(1)} %get-tuple-element.4.ana_t_ref, ...), custom_call_target="tpu_custom_call" | custom-call | tf_op jit(solution)/shard_map/pallas_call | solution.py:252
  77.2 0.0 all-to-all-done.1
  77.3 0.0 copy-done.1
  77.3 1.2 %fusion.1 = f32[1,16,32,128]{3,2,1,0:T(8,128)} fusion(f32[16,12,128]{2,1,0:T(8,128)S(1)} %all-to-all-done.1, f32[1,16,64,128]{3,2,1,0:T(8,128)S(1)} %copy-done.1, s32[]{:T(128)S(6)} %select_n.81, f32[64,12]{0,1:T(8,128)S(1)} %fusion.21), kind=kOutput, calls=%fused_computation.2 | convolution fusion | flops 9502720 | bytes 626688 | tf_op jit(solution)/shard_map/sc,zcx->zsx/dot_general | solution.py:211
  (4 shorter events, 0.0 us)
Async XLA Ops:
  2.3 0.7 copy-start.4
  5.2 7.6 %copy-start.2 = (f32[16,64,6]{1,0,2:T(8,128)S(1)}, f32[16,64,6]{1,0,2:T(8,128)}, u32[]{:S(2)}) copy-start(f32[16,64,6]{1,0,2:T(8,128)} %param.8) | copy-start | bytes 73732
  5.2 40.8 %all-to-all-start = ((f32[16,7,128]{2,1,0:T(8,128)}), f32[16,7,128]{2,1,0:T(8,128)S(1)}, u32[]{:S(2)}, u32[]{:S(2)}) async-start(f32[16,7,128]{2,1,0:T(8,128)} %concatenate.3), calls=%async_computation | async-start | bytes 131072 | tf_op jit(solution)/shard_map/all_to_all | solution.py:234
  17.9 1.8 %copy-start = (bf16[1,6,128,128]{3,2,1,0:T(8,128)(2,1)S(1)}, bf16[1,6,128,128]{3,2,1,0:T(8,128)(2,1)}, u32[]{:S(2)}) copy-start(bf16[1,6,128,128]{3,2,1,0:T(8,128)(2,1)} %param.6) | copy-start | bytes 589828
  19.0 0.7 copy-start.3
  47.7 29.6 %all-to-all-start.1 = ((f32[16,12,128]{2,1,0:T(8,128)}), f32[16,12,128]{2,1,0:T(8,128)S(1)}, u32[]{:S(2)}, u32[]{:S(2)}) async-start(f32[16,12,128]{2,1,0:T(8,128)} %copy.27), calls=%async_computation.1 | async-start | bytes 262144 | tf_op jit(solution)/shard_map/all_to_all | solution.py:261
  53.7 23.6 %copy-start.1 = (f32[1,16,64,128]{3,2,1,0:T(8,128)S(1)}, f32[1,16,64,128]{3,2,1,0:T(8,128)}, u32[]{:S(2)}) copy-start(f32[1,16,64,128]{3,2,1,0:T(8,128)} %param.7) | copy-start | bytes 1572868

commit v2 on v1

--- a/solution.py
+++ b/solution.py
@@ -158,114 +158,243 @@
             )
 
 
-def forward_kernel(
-    volume_ref, angle_ref, ana_ref, ana_t_ref, syn_ref, out_ref, unit_ref, spec_ref, row_ref, col_ref, mix_ref
+MESH = pl.DeviceIdType.MESH
+LIMIT = 48 << 20
+
+
+def exact(left, right, contract=((1,), (0,))):
+    return lax.dot_general(
+        left, right, (contract, ((), ())), precision=lax.Precision.HIGHEST, preferred_element_type=WIDE
+    )
+
+
+def whole_kernel(
+    orients, coefs, own_coefs,
+    volume_ref, data_ref, basis_ref, angle_ref, index_ref, map_ref, ana_ref, ana_t_ref, syn_ref, syn_t_ref,
+    grad_ref, resid_ref,
+    unit_ref, spec_ref, row_ref, col_ref, mix_ref, total_ref,
+    basis_all, pull_out, pull_in, prof_all, back_out, back_in,
+    basis_send, basis_recv, pull_send, pull_recv, prof_send, prof_recv, back_send, back_recv,
 ):
+    me, mine = lax.axis_index("orient"), lax.axis_index("coef")
     images, grid_size = volume_ref.shape[0], volume_ref.shape[-1]
+    tables, padded, segs = basis_ref.shape
+    planes = data_ref.shape[0]
+    share = resid_ref.shape[1]
+
+    def ahead(step):
+        return lax.rem(me + step, orients)
+
+    def behind(step):
+        return lax.rem(me + orients - step, orients)
+
+    def basis_copy(step):
+        return pltpu.make_async_remote_copy(
+            src_ref=basis_ref, dst_ref=basis_all.at[mine],
+            send_sem=basis_send.at[step - 1], recv_sem=basis_recv.at[step - 1],
+            device_id=(me, lax.rem(mine + step, coefs)), device_id_type=MESH,
+        )
+
+    def prof_copy(step, which):
+        return pltpu.make_async_remote_copy(
+            src_ref=prof_all.at[which, mine], dst_ref=prof_all.at[which, mine],
+            send_sem=prof_send.at[step - 1, which], recv_sem=prof_recv.at[step - 1, which],
+            device_id=(me, lax.rem(mine + step, coefs)), device_id_type=MESH,
+        )
+
+    def pull_copy(step):
+        return pltpu.make_async_remote_copy(
+            src_ref=pull_out.at[ahead(step)], dst_ref=pull_in.at[me],
+            send_sem=pull_send.at[step - 1], recv_sem=pull_recv.at[step - 1],
+            device_id=(ahead(step), mine), device_id_type=MESH,
+        )
+
+    def back_copy(step):
+        return pltpu.make_async_remote_copy(
+            src_ref=back_out.at[ahead(step)], dst_ref=back_in.at[me],
+            send_sem=back_send.at[step - 1], recv_sem=back_recv.at[step - 1],
+            device_id=(ahead(step), mine), device_id_type=MESH,
+        )
+
+    def over_steps(action):
+        def one(step, carry):
+            action(step)
+            return carry
+
+        lax.fori_loop(1, orients, one, 0)
+
+    barrier = pltpu.get_barrier_semaphore()
+    over_steps(
+        lambda step: pl.semaphore_signal(
+            barrier, inc=1, device_id=(ahead(step), mine), device_id_type=MESH
+        )
+    )
+    for step in range(1, coefs):
+        pl.semaphore_signal(
+            barrier, inc=1, device_id=(me, lax.rem(mine + step, coefs)), device_id_type=MESH
+        )
+
+    map_row = map_ref[...]
+    chosen = (lax.broadcasted_iota(jnp.int32, (segs, segs), 0) == map_row).astype(WIDE)
+    index = index_ref[0]
+    own_mix_t = exact(basis_ref[index], chosen)
+    tag_row = lax.broadcasted_iota(jnp.int32, (padded, grid_size), 0) == own_coefs
+    tag = index.astype(WIDE)
+
+    def pull_one(plane, carry):
+        pull_out[plane] = jnp.where(tag_row, tag, exact(own_mix_t, data_ref[plane]))
+        return carry
+
+    lax.fori_loop(0, planes, pull_one, 0, unroll=4)
+    pull_in[me] = pull_out[me]
+    basis_all[mine] = basis_ref[...]
+    pl.semaphore_wait(barrier, orients + coefs - 2)
+    for step in range(1, coefs):
+        basis_copy(step).start()
+    over_steps(lambda step: pull_copy(step).start())
+
     unit_waves(angle_ref[...], grid_size, unit_ref)
     volume_spectra(volume_ref, ana_t_ref[...], spec_ref, images, grid_size)
-
-    def step(which, carry):
-        build_tables(which, grid_size, unit_ref, row_ref, col_ref, mix_ref, 0, syn_ref[...])
+    filler = jnp.zeros((padded - images, grid_size), WIDE)
+
+    def project(which, carry):
+        build_tables(which, grid_size, unit_ref, row_ref, col_ref, mix_ref, which, syn_ref[...])
         waves = (ana_ref[...], ana_t_ref[...], syn_ref[...])
-        out_ref[which] = forward_one(0, images, grid_size, spec_ref, row_ref, col_ref, mix_ref, waves)
-        return carry
-
-    lax.fori_loop(0, out_ref.shape[0], step, 0)
-
-
-def backward_kernel(
-    rows_ref, angle_ref, ana_ref, ana_t_ref, syn_ref, syn_t_ref, out_ref, unit_ref, total_ref, row_ref, col_ref, mix_ref
-):
-    images, grid_size = out_ref.shape[0], out_ref.shape[-1]
-    unit_waves(angle_ref[...], grid_size, unit_ref)
+        rows = forward_one(which, images, grid_size, spec_ref, row_ref, col_ref, mix_ref, waves)
+        prof_all[which, mine] = jnp.concatenate([rows, filler], axis=0)
+        for step in range(1, coefs):
+            prof_copy(step, which).start()
+        return carry
+
+    lax.fori_loop(0, tables, project, 0)
+
     total_ref[...] = jnp.zeros_like(total_ref)
-
-    def step(which, carry):
-        build_tables(which, grid_size, unit_ref, row_ref, col_ref, mix_ref, 0, syn_ref[...])
+    for step in range(1, coefs):
+        basis_copy(step).wait()
+    over_steps(lambda step: pull_copy(step).wait())
+
+    def arrived(which, carry):
+        for step in range(1, coefs):
+            prof_copy(step, which).wait()
+        return carry
+
+    def spread_back(which, carry):
+        rows = jnp.zeros((padded, grid_size), WIDE)
+        for orient in range(orients):
+            block = pull_in[orient]
+            tags = block[own_coefs : own_coefs + 1]
+            rows = rows - jnp.where(tags == which.astype(WIDE), block, 0.0)
+        for part in range(coefs):
+            gram = exact(basis_ref[which], basis_all[part, which], ((1,), (1,)))
+            rows = rows + exact(gram, prof_all[which, part])
         waves = (ana_ref[...], ana_t_ref[...], syn_t_ref[...])
         backward_one(
-            0, rows_ref[which].astype(NARROW), grid_size, total_ref, row_ref, col_ref, mix_ref, waves
-        )
-        return carry
-
-    lax.fori_loop(0, rows_ref.shape[0], step, 0)
+            which, rows[:images].astype(NARROW), grid_size, total_ref, row_ref, col_ref, mix_ref, waves
+        )
+        return carry
+
+    early = tables // 2
+    lax.fori_loop(0, early, lambda which, carry: spread_back(which, arrived(which, carry)), 0)
+    lax.fori_loop(early, tables, arrived, 0)
+
+    def return_one(orient, carry):
+        tags = pull_in[orient][own_coefs : own_coefs + 1]
+
+        def add(which, found):
+            return found + jnp.where(tags[None] == which.astype(WIDE), prof_all[which], 0.0)
+
+        back_out[orient] = lax.fori_loop(
+            0, tables, add, jnp.zeros((coefs, padded, grid_size), WIDE), unroll=8
+        )
+        return carry
+
+    lax.fori_loop(0, orients, return_one, 0)
+    back_in[me] = back_out[me]
+    over_steps(lambda step: back_copy(step).start())
+    lax.fori_loop(early, tables, spread_back, 0)
     for image in range(images):
-        out_ref[image] = mul(total_ref[image].astype(NARROW), ana_ref[...])
-
-
-VMEM = functools.partial(pl.BlockSpec, memory_space=pltpu.VMEM)
-LIMIT = 40 << 20
-
-
-def table_scratch(count, grid_size, slots):
-    return [
-        pltpu.VMEM((4, count, grid_size), WIDE),
-        pltpu.VMEM((slots, 2, grid_size, grid_size), WIDE),
-        pltpu.VMEM((slots, 2, grid_size, grid_size), WIDE),
-        pltpu.VMEM((slots, 2, grid_size, grid_size), WIDE),
-    ]
-
-
-def exact(pattern, left, right):
-    return jnp.einsum(pattern, left, right, precision=lax.Precision.HIGHEST)
+        grad_ref[image] = mul(total_ref[image].astype(NARROW), ana_ref[...])
+
+    row_ids = lax.broadcasted_iota(jnp.int32, (share, segs), 0) + mine * share
+    lane_ids = lax.broadcasted_iota(jnp.int32, (share, segs), 1)
+    map_column = jnp.sum(
+        jnp.where(row_ids == lane_ids, map_row.astype(WIDE), 0.0), axis=1, keepdims=True
+    )
+    picked = (lane_ids.astype(WIDE) == map_column).astype(WIDE)
+    all_basis = jnp.concatenate([basis_all[part, index] for part in range(coefs)], axis=0)
+    share_mix = exact(picked, all_basis, ((1,), (1,)))
+    start = pl.multiple_of(mine * share, share)
+    over_steps(lambda step: back_copy(step).wait())
+
+    def residual_one(plane, carry):
+        rows = back_in[plane].reshape(coefs * padded, grid_size)
+        resid_ref[plane] = exact(share_mix, rows) - data_ref[plane, pl.ds(start, share), :]
+        return carry
+
+    lax.fori_loop(0, planes, residual_one, 0, unroll=4)
 
 
 def body(volume, measured, basis_table, angle_table, angle_index, sector_map):
     grid_size = volume.shape[-1]
     images = volume.shape[0] * volume.shape[1]
     own_coefs = basis_table.shape[2]
-    table_count = angle_table.shape[0]
-    seg_count = measured.shape[2]
-    seg_share = seg_count // lax.axis_size("coef")
+    tables = angle_table.shape[0]
+    planes, segs = measured.shape[1], measured.shape[2]
+    orients, coefs = lax.axis_size("orient"), lax.axis_size("coef")
+    share = segs // coefs
+    padded = (own_coefs + 8) // 8 * 8
     analysis, synthesis = dft_tables(grid_size)
-    angles = jnp.broadcast_to(angle_table[:, None], (table_count, grid_size))
-    unit_s, row_s, col_s, mix_s = table_scratch(table_count, grid_size, 1)
-
-    table_ids = jnp.arange(table_count, dtype=jnp.int32)
-    own_hot = (angle_index[0] == table_ids).astype(WIDE)
-    permute = (sector_map[0][:, None] == jnp.arange(seg_count, dtype=jnp.int32)).astype(WIDE)
-    own_mix = exact("st,tc->sc", permute, exact("a,asc->sc", own_hot, basis_table))
-    pulled = exact("zsx,sc->zcx", measured[0], own_mix)
-    tagged = jnp.concatenate(
-        [pulled, jnp.broadcast_to(angle_index[0].astype(WIDE), (pulled.shape[0], 1, grid_size))],
-        axis=1,
-    )
-    arrived = lax.all_to_all(tagged, "orient", split_axis=0, concat_axis=0, tiled=True)
-    basis_full = lax.all_gather(basis_table, "coef", axis=2, tiled=True)
-
-    profiles = pl.pallas_call(
-        forward_kernel,
-        out_shape=jax.ShapeDtypeStruct((table_count, images, grid_size), WIDE),
-        in_specs=[VMEM()] * 5,
-        out_specs=VMEM(),
-        scratch_shapes=[unit_s, pltpu.VMEM((2, images, grid_size, grid_size), WIDE), row_s, col_s, mix_s],
-        compiler_params=pltpu.CompilerParams(vmem_limit_bytes=LIMIT),
-    )(volume.reshape(images, grid_size, grid_size), angles, analysis, analysis.T, synthesis)
-
-    all_profiles = lax.all_gather(profiles, "coef", axis=1, tiled=True)
-    hot = (arrived[:, own_coefs, 0].astype(jnp.int32)[:, None] == table_ids).astype(WIDE)
-    gram = exact("asc,asd->acd", basis_table, basis_full)
-    contracted = exact("acd,adx->acx", gram, all_profiles) - exact(
-        "oa,ocx->acx", hot, arrived[:, :own_coefs]
-    )
-    gradient = pl.pallas_call(
-        backward_kernel,
-        out_shape=jax.ShapeDtypeStruct((images, grid_size, grid_size), WIDE),
-        in_specs=[VMEM()] * 6,
-        out_specs=VMEM(),
-        scratch_shapes=[unit_s, pltpu.VMEM((images, grid_size, grid_size), WIDE), row_s, col_s, mix_s],
-        compiler_params=pltpu.CompilerParams(vmem_limit_bytes=LIMIT),
-    )(contracted, angles, analysis, analysis.T, synthesis, synthesis.T)
-
-    returned = lax.all_to_all(
-        exact("oa,acx->ocx", hot, all_profiles), "orient", split_axis=0, concat_axis=0, tiled=True
-    )
-    full_mix = exact("st,tc->sc", permute, exact("a,asc->sc", own_hot, basis_full))
-    start_seg = lax.axis_index("coef") * seg_share
-    share_mix = lax.dynamic_slice_in_dim(full_mix, start_seg, seg_share, 0)
-    share_data = lax.dynamic_slice_in_dim(measured[0], start_seg, seg_share, 1)
-    residual = exact("sc,zcx->zsx", share_mix, returned) - share_data
+    angles = jnp.broadcast_to(angle_table[:, None], (tables, grid_size))
+    basis = jnp.pad(basis_table.transpose(0, 2, 1), ((0, 0), (0, padded - own_coefs), (0, 0)))
+    vmem = pl.BlockSpec(memory_space=pltpu.VMEM)
+    smem = pl.BlockSpec(memory_space=pltpu.SMEM)
+    table = pltpu.VMEM((tables, 2, grid_size, grid_size), WIDE)
+    dma = pltpu.SemaphoreType.DMA
+    gradient, residual = pl.pallas_call(
+        functools.partial(whole_kernel, orients, coefs, own_coefs),
+        out_shape=(
+            jax.ShapeDtypeStruct((images, grid_size, grid_size), WIDE),
+            jax.ShapeDtypeStruct((planes, share, grid_size), WIDE),
+        ),
+        in_specs=[vmem] * 4 + [smem] + [vmem] * 5,
+        out_specs=(vmem, vmem),
+        scratch_shapes=[
+            pltpu.VMEM((4, tables, grid_size), WIDE),
+            pltpu.VMEM((2, images, grid_size, grid_size), WIDE),
+            table,
+            table,
+            table,
+            pltpu.VMEM((images, grid_size, grid_size), WIDE),
+            pltpu.VMEM((coefs, tables, padded, segs), WIDE),
+            pltpu.VMEM((planes, padded, grid_size), WIDE),
+            pltpu.VMEM((orients, padded, grid_size), WIDE),
+            pltpu.VMEM((tables, coefs, padded, grid_size), WIDE),
+            pltpu.VMEM((orients, coefs, padded, grid_size), WIDE),
+            pltpu.VMEM((planes, coefs, padded, grid_size), WIDE),
+            dma((coefs - 1,)),
+            dma((coefs - 1,)),
+            dma((orients - 1,)),
+            dma((orients - 1,)),
+            dma((coefs - 1, tables)),
+            dma((coefs - 1, tables)),
+            dma((orients - 1,)),
+            dma((orients - 1,)),
+        ],
+        compiler_params=pltpu.CompilerParams(
+            collective_id=0, has_side_effects=True, vmem_limit_bytes=LIMIT
+        ),
+    )(
+        volume.reshape(images, grid_size, grid_size),
+        measured[0],
+        basis,
+        angles,
+        angle_index,
+        sector_map,
+        analysis,
+        analysis.T,
+        synthesis,
+        synthesis.T,
+    )
     return (gradient.reshape(volume.shape), residual[None])
 
 

time: 78.9 us -> 65.9 us (0.84)
  Pallas kernels: 44.8 us -> 59 us
  starting transfers between devices: 13.5 us -> 0 us
  blocking collectives: 9.53 us -> 0 us
  matrix products: 5.24 us -> 0 us
  local copies, waits for them, and re-layouts: 2.95 us -> 4.71 us
    pallas_call x2 -> x1, Pallas kernels: 44.8 us -> 59 us  [body(): pl.pallas_call(functools.partial(whole_kernel, orients, coefs, own_coefs)...]
    all_to_all x2 -> x0, starting transfers between devices: 13.5 us -> none  [the longest x1 7.52 us: body(): lax.all_to_all(tagged, 'orient', split_axis=0, concat_axis=0, tiled=True)]
    all_gather x2 -> x0, blocking collectives: 9.53 us -> none  [the longest x1 4.77 us: body(): basis_full = lax.all_gather(basis_table, 'coef', axis=2, tiled=True)]
    dot_general x10 -> x0, matrix products: 5.24 us -> none  [exact(): return jnp.einsum(pattern, left, right, precision=lax.Precision.HIGHEST)]
    unnamed x10 -> x11, local copies, waits for them, and re-layouts: 1.35 us -> 4.63 us
    dot_general x3 -> x0, local copies, waits for them, and re-layouts: 0.88 us -> none  [exact(): return jnp.einsum(pattern, left, right, precision=lax.Precision.HIGHEST)]
  transfers between devices with their start and end apart: 2 -> 0, of which waited for: 0 -> 0; matrix products, arithmetic and copies ran while one was open for 2% -> 0% of each run, Pallas kernels for 57% -> 0%
where the time goes in v2:
time: 65.9 us; the launch traced here: 65.7 us
  Pallas kernels  59 us (90%)
  local copies, waits for them, and re-layouts  4.71 us (7%)
  between operations  1.35 us (2%)
    pallas_call x1, Pallas kernels, body(): pl.pallas_call(functools.partial(whole_kernel, orients, coefs, own_coefs)...  59 us
    unnamed x11, local copies, waits for them, and re-layouts  4.63 us

profile of v2, /device:TPU:0, one launch (start us, length us, event | category | flops | bytes accessed | tf_op | source)
XLA Modules:
  0.0 65.7 jit_solution(2933704968513287622)
XLA Ops:
  1.3 0.0 copy-start.3
  1.3 0.6 copy-done.3
  2.0 0.1 broadcast_in_dim.35.angle_ref
  2.0 0.0 copy-start.1
  2.0 0.9 %copy.10 = f32[16,64,6]{1,2,0:T(8,128)S(1)} copy(f32[16,64,6]{1,0,2:T(8,128)} %param.8) | data formatting | bytes 49152 | tf_op args[2]
  2.9 0.6 multiply_convert_fusion
  3.5 0.0 copy-start.2
  3.5 0.0 copy-done.1
  3.5 0.6 copy-done.2
  4.2 0.0 copy-start
  4.2 1.0 %copy-done = f32[1,16,64,128]{3,2,1,0:T(8,128)S(1)} copy-done((f32[1,16,64,128]{3,2,1,0:T(8,128)S(1)}, f32[1,16,64,128]{3,2,1,0:T(8,128)}, u32[]{:S(2)}) %copy-start) | copy-done | bytes 524312
  5.2 59.0 %shard_map.77 = (f32[6,128,128]{2,1,0:T(8,128)S(1)}, f32[16,32,128]{2,1,0:T(8,128)S(1)}) custom-call(bf16[6,128,128]{2,1,0:T(8,128)(2,1)S(1)} %bitcast.10, f32[16,64,128]{2,1,0:T(8,128)S(1)} %bitcast.7, f32[16,8,64]{2,1,0:T(8,128)S(1)} %pad.4.basis_ref, f32[16,128]{1,0:T(8,128)S(1)} %broadcast_in_dim.35.angle_ref, s32[1]{0:T(128)S(6)} %copy.13.index_ref, ...), custom_call_target="tpu_custom_call" | custom-call | tf_op jit(solution)/shard_map/pallas_call | solution.py:353
  64.2 0.7 %copy.14 = f32[1,6,128,128]{3,2,1,0:T(8,128)} copy(f32[1,6,128,128]{3,2,1,0:T(8,128)S(1)} %bitcast.8) | data formatting | bytes 786432
  65.0 0.7 %copy.15 = f32[1,16,32,128]{3,2,1,0:T(8,128)} copy(f32[1,16,32,128]{3,2,1,0:T(8,128)S(1)} %bitcast.9) | data formatting | bytes 524288
  (4 shorter events, 0.0 us)
Async XLA Ops:
  1.3 0.7 %copy-start.3 = (f32[16]{0:T(128)S(1)}, f32[16]{0:T(128)}, u32[]{:S(2)}) copy-start(f32[16]{0:T(128)} %param.9) | copy-start | bytes 196
  2.0 1.5 %copy-start.1 = (bf16[1,6,128,128]{3,2,1,0:T(8,128)(2,1)S(1)}, bf16[1,6,128,128]{3,2,1,0:T(8,128)(2,1)}, u32[]{:S(2)}) copy-start(bf16[1,6,128,128]{3,2,1,0:T(8,128)(2,1)} %param.6) | copy-start | bytes 589828
  3.5 0.7 %copy-start.2 = (s32[1,64]{1,0:T(1,128)S(1)}, s32[1,64]{1,0:T(1,128)}, u32[]{:S(2)}) copy-start(s32[1,64]{1,0:T(1,128)} %map_ref.1) | copy-start | bytes 772
  4.2 1.0 %copy-start = (f32[1,16,64,128]{3,2,1,0:T(8,128)S(1)}, f32[1,16,64,128]{3,2,1,0:T(8,128)}, u32[]{:S(2)}) copy-start(f32[1,16,64,128]{3,2,1,0:T(8,128)} %param.7) | copy-start | bytes 1572868

commit v3 on v2

--- a/solution.py
+++ b/solution.py
@@ -113,49 +113,64 @@
         spec_ref[1, image] = pltpu.roll(spectrum, grid_size // 2, 1)
 
 
-def forward_one(slot, images, grid_size, spec_ref, row_ref, col_ref, mix_ref, waves):
+def forward_pair(slot, images, grid_size, spec_ref, sides, waves):
     analysis, analysis_t, synthesis = waves
-    sums, rolled = [], []
+    half = grid_size // 2
+    sums, rolled = [[] for _ in sides], [[] for _ in sides]
     for group in image_groups(images):
-        fields = []
-        for image in group:
-            turned = spec_ref[0, image] * row_ref[slot, 0] + spec_ref[1, image] * row_ref[slot, 1]
-            fields.append(mul(turned.astype(NARROW), synthesis).astype(NARROW))
-        spectrum = mul(analysis, jnp.concatenate(fields, axis=1))
-        for at in range(len(group)):
-            own = spectrum[:, at * grid_size : (at + 1) * grid_size]
-            turned = own * col_ref[slot, 0] + swap_rows(own) * col_ref[slot, 1]
-            last = mul(turned.astype(NARROW), analysis_t)
-            sums.append(jnp.sum(last * mix_ref[slot, 0], axis=0, keepdims=True))
-            rolled.append(jnp.sum(last * mix_ref[slot, 1], axis=0, keepdims=True))
-    total = jnp.concatenate(sums, axis=0)
-    crossed = pltpu.roll(jnp.concatenate(rolled, axis=0), grid_size // 2, 1)
-    summed = (total - crossed).astype(NARROW)
-    return mul(summed, synthesis) * (1.0 / math.sqrt(grid_size))
-
-
-def backward_one(slot, rows, grid_size, total_ref, row_ref, col_ref, mix_ref, waves):
+        spectra = []
+        for row_ref, _, _ in sides:
+            fields = []
+            for image in group:
+                turned = (
+                    spec_ref[0, image] * row_ref[slot, 0] + spec_ref[1, image] * row_ref[slot, 1]
+                )
+                fields.append(mul(turned.astype(NARROW), synthesis).astype(NARROW))
+            spectra.append(mul(analysis, jnp.concatenate(fields, axis=1)))
+        for side, (_, col_ref, mix_ref) in enumerate(sides):
+            for at in range(len(group)):
+                own = spectra[side][:, at * grid_size : (at + 1) * grid_size]
+                turned = own * col_ref[slot, 0] + swap_rows(own) * col_ref[slot, 1]
+                last = mul(turned.astype(NARROW), analysis_t)
+                sums[side].append(jnp.sum(last * mix_ref[slot, 0], axis=0, keepdims=True))
+                rolled[side].append(jnp.sum(last * mix_ref[slot, 1], axis=0, keepdims=True))
+    profiles = []
+    for side in range(len(sides)):
+        total = jnp.concatenate(sums[side], axis=0)
+        crossed = pltpu.roll(jnp.concatenate(rolled[side], axis=0), half, 1)
+        summed = (total - crossed).astype(NARROW)
+        profiles.append(mul(summed, synthesis) * (1.0 / math.sqrt(grid_size)))
+    return profiles
+
+
+def backward_pair(slot, spectra, images, grid_size, total_ref, sides, waves):
     analysis, analysis_t, synthesis_t = waves
-    images = rows.shape[0]
-    spectra = mul(rows, synthesis_t) * (1.0 / math.sqrt(grid_size))
-    crossed = pltpu.roll(spectra, grid_size // 2, 1)
+    half = grid_size // 2
     for group in image_groups(images):
-        fields = []
-        for image in group:
-            spread = (
-                spectra[image : image + 1] * mix_ref[slot, 0]
-                - crossed[image : image + 1] * mix_ref[slot, 1]
-            )
-            own = mul(spread.astype(NARROW), analysis)
-            turned = own * col_ref[slot, 0] - swap_rows(own) * col_ref[slot, 1]
-            fields.append(turned.astype(NARROW))
-        field = mul(analysis_t, jnp.concatenate(fields, axis=1)).astype(NARROW)
+        spread_out = []
+        for (own_rows, crossed), (_, col_ref, mix_ref) in zip(spectra, sides):
+            fields = []
+            for image in group:
+                spread = (
+                    own_rows[image : image + 1] * mix_ref[slot, 0]
+                    - crossed[image : image + 1] * mix_ref[slot, 1]
+                )
+                own = mul(spread.astype(NARROW), analysis)
+                turned = own * col_ref[slot, 0] - swap_rows(own) * col_ref[slot, 1]
+                fields.append(turned.astype(NARROW))
+            spread_out.append(mul(analysis_t, jnp.concatenate(fields, axis=1)).astype(NARROW))
         for at, image in enumerate(group):
-            own = mul(field[:, at * grid_size : (at + 1) * grid_size], synthesis_t)
-            total_ref[image] += (
-                own * row_ref[slot, 0]
-                - pltpu.roll(own, grid_size // 2, 1) * row_ref[slot, 1]
-            )
+            added = None
+            for field, (row_ref, _, _) in zip(spread_out, sides):
+                own = mul(field[:, at * grid_size : (at + 1) * grid_size], synthesis_t)
+                turned = own * row_ref[slot, 0] - pltpu.roll(own, half, 1) * row_ref[slot, 1]
+                added = turned if added is None else added + turned
+            total_ref[image] += added
+
+
+def split(value):
+    high = value.astype(NARROW)
+    return high, (value - high.astype(WIDE)).astype(NARROW)
 
 
 MESH = pl.DeviceIdType.MESH
@@ -172,7 +187,7 @@
     orients, coefs, own_coefs,
     volume_ref, data_ref, basis_ref, angle_ref, index_ref, map_ref, ana_ref, ana_t_ref, syn_ref, syn_t_ref,
     grad_ref, resid_ref,
-    unit_ref, spec_ref, row_ref, col_ref, mix_ref, total_ref,
+    unit_ref, spec_ref, row_a, col_a, mix_a, row_b, col_b, mix_b, total_ref,
     basis_all, pull_out, pull_in, prof_all, back_out, back_in,
     basis_send, basis_recv, pull_send, pull_recv, prof_send, prof_recv, back_send, back_recv,
 ):
@@ -234,6 +249,9 @@
             barrier, inc=1, device_id=(me, lax.rem(mine + step, coefs)), device_id_type=MESH
         )
 
+    unit_waves(angle_ref[...], grid_size, unit_ref)
+    volume_spectra(volume_ref, ana_t_ref[...], spec_ref, images, grid_size)
+    total_ref[...] = jnp.zeros_like(total_ref)
     map_row = map_ref[...]
     chosen = (lax.broadcasted_iota(jnp.int32, (segs, segs), 0) == map_row).astype(WIDE)
     index = index_ref[0]
@@ -241,11 +259,14 @@
     tag_row = lax.broadcasted_iota(jnp.int32, (padded, grid_size), 0) == own_coefs
     tag = index.astype(WIDE)
 
+    mix_parts = jnp.concatenate(split(own_mix_t), axis=0)
+
     def pull_one(plane, carry):
-        pull_out[plane] = jnp.where(tag_row, tag, exact(own_mix_t, data_ref[plane]))
+        both = mul(mix_parts, data_ref[plane].astype(NARROW))
+        pull_out[plane] = jnp.where(tag_row, tag, both[:padded] + both[padded:])
         return carry
 
-    lax.fori_loop(0, planes, pull_one, 0, unroll=4)
+    lax.fori_loop(0, planes, pull_one, 0, unroll=8)
     pull_in[me] = pull_out[me]
     basis_all[mine] = basis_ref[...]
     pl.semaphore_wait(barrier, orients + coefs - 2)
@@ -253,49 +274,65 @@
         basis_copy(step).start()
     over_steps(lambda step: pull_copy(step).start())
 
-    unit_waves(angle_ref[...], grid_size, unit_ref)
-    volume_spectra(volume_ref, ana_t_ref[...], spec_ref, images, grid_size)
     filler = jnp.zeros((padded - images, grid_size), WIDE)
 
-    def project(which, carry):
-        build_tables(which, grid_size, unit_ref, row_ref, col_ref, mix_ref, which, syn_ref[...])
+    sides = ((row_a, col_a, mix_a), (row_b, col_b, mix_b))
+    pairs = tables // 2
+
+    def project(slot, carry):
+        for side, refs in enumerate(sides):
+            build_tables(2 * slot + side, grid_size, unit_ref, *refs, slot, syn_ref[...])
         waves = (ana_ref[...], ana_t_ref[...], syn_ref[...])
-        rows = forward_one(which, images, grid_size, spec_ref, row_ref, col_ref, mix_ref, waves)
-        prof_all[which, mine] = jnp.concatenate([rows, filler], axis=0)
-        for step in range(1, coefs):
-            prof_copy(step, which).start()
+        profiles = forward_pair(slot, images, grid_size, spec_ref, sides, waves)
+        for side, rows in enumerate(profiles):
+            prof_all[2 * slot + side, mine] = jnp.concatenate([rows, filler], axis=0)
+        for side in range(2):
+            for step in range(1, coefs):
+                prof_copy(step, 2 * slot + side).start()
         return carry
 
-    lax.fori_loop(0, tables, project, 0)
-
-    total_ref[...] = jnp.zeros_like(total_ref)
+    lax.fori_loop(0, pairs, project, 0)
+
     for step in range(1, coefs):
         basis_copy(step).wait()
     over_steps(lambda step: pull_copy(step).wait())
 
-    def arrived(which, carry):
-        for step in range(1, coefs):
-            prof_copy(step, which).wait()
+    def arrived(slot, carry):
+        for side in range(2):
+            for step in range(1, coefs):
+                prof_copy(step, 2 * slot + side).wait()
         return carry
 
-    def spread_back(which, carry):
-        rows = jnp.zeros((padded, grid_size), WIDE)
-        for orient in range(orients):
-            block = pull_in[orient]
-            tags = block[own_coefs : own_coefs + 1]
-            rows = rows - jnp.where(tags == which.astype(WIDE), block, 0.0)
-        for part in range(coefs):
-            gram = exact(basis_ref[which], basis_all[part, which], ((1,), (1,)))
-            rows = rows + exact(gram, prof_all[which, part])
+    def contract(slot):
+        found = []
+        for side in range(2):
+            which = 2 * slot + side
+            rows = jnp.zeros((padded, grid_size), WIDE)
+            for orient in range(orients):
+                block = pull_in[orient]
+                tags = block[own_coefs : own_coefs + 1]
+                rows = rows - jnp.where(tags == lax.convert_element_type(which, WIDE), block, 0.0)
+            for part in range(coefs):
+                gram = exact(basis_ref[which], basis_all[part, which], ((1,), (1,)))
+                rows = rows + exact(gram, prof_all[which, part])
+            spectra = mul(rows.astype(NARROW), syn_t_ref[...]) * (1.0 / math.sqrt(grid_size))
+            found.append((spectra, pltpu.roll(spectra, grid_size // 2, 1)))
+        return tuple(found)
+
+    def spread_back(slot, spectra):
         waves = (ana_ref[...], ana_t_ref[...], syn_t_ref[...])
-        backward_one(
-            which, rows[:images].astype(NARROW), grid_size, total_ref, row_ref, col_ref, mix_ref, waves
-        )
-        return carry
-
-    early = tables // 2
-    lax.fori_loop(0, early, lambda which, carry: spread_back(which, arrived(which, carry)), 0)
-    lax.fori_loop(early, tables, arrived, 0)
+        following = contract(jnp.minimum(slot + 1, pairs - 1))
+        backward_pair(slot, spectra, images, grid_size, total_ref, sides, waves)
+        return following
+
+    def first_part(slot, spectra):
+        arrived(slot + 1, 0)
+        return spread_back(slot, spectra)
+
+    early = pairs // 2
+    arrived(0, 0)
+    spectra = lax.fori_loop(0, early, first_part, contract(jnp.int32(0)))
+    lax.fori_loop(early + 1, pairs, arrived, 0)
 
     def return_one(orient, carry):
         tags = pull_in[orient][own_coefs : own_coefs + 1]
@@ -304,14 +341,14 @@
             return found + jnp.where(tags[None] == which.astype(WIDE), prof_all[which], 0.0)
 
         back_out[orient] = lax.fori_loop(
-            0, tables, add, jnp.zeros((coefs, padded, grid_size), WIDE), unroll=8
+            0, tables, add, jnp.zeros((coefs, padded, grid_size), WIDE), unroll=16
         )
         return carry
 
     lax.fori_loop(0, orients, return_one, 0)
     back_in[me] = back_out[me]
     over_steps(lambda step: back_copy(step).start())
-    lax.fori_loop(early, tables, spread_back, 0)
+    lax.fori_loop(early, pairs, spread_back, spectra)
     for image in range(images):
         grad_ref[image] = mul(total_ref[image].astype(NARROW), ana_ref[...])
 
@@ -322,16 +359,19 @@
     )
     picked = (lane_ids.astype(WIDE) == map_column).astype(WIDE)
     all_basis = jnp.concatenate([basis_all[part, index] for part in range(coefs)], axis=0)
-    share_mix = exact(picked, all_basis, ((1,), (1,)))
+    high, low = split(exact(picked, all_basis, ((1,), (1,))))
+    share_mix = jnp.concatenate([high, low, high], axis=1)
     start = pl.multiple_of(mine * share, share)
     over_steps(lambda step: back_copy(step).wait())
 
     def residual_one(plane, carry):
         rows = back_in[plane].reshape(coefs * padded, grid_size)
-        resid_ref[plane] = exact(share_mix, rows) - data_ref[plane, pl.ds(start, share), :]
+        high, low = split(rows)
+        signals = mul(share_mix, jnp.concatenate([high, high, low], axis=0))
+        resid_ref[plane] = signals - data_ref[plane, pl.ds(start, share), :]
         return carry
 
-    lax.fori_loop(0, planes, residual_one, 0, unroll=4)
+    lax.fori_loop(0, planes, residual_one, 0, unroll=8)
 
 
 def body(volume, measured, basis_table, angle_table, angle_index, sector_map):
@@ -348,7 +388,7 @@
     basis = jnp.pad(basis_table.transpose(0, 2, 1), ((0, 0), (0, padded - own_coefs), (0, 0)))
     vmem = pl.BlockSpec(memory_space=pltpu.VMEM)
     smem = pl.BlockSpec(memory_space=pltpu.SMEM)
-    table = pltpu.VMEM((tables, 2, grid_size, grid_size), WIDE)
+    table = pltpu.VMEM((tables // 2, 2, grid_size, grid_size), WIDE)
     dma = pltpu.SemaphoreType.DMA
     gradient, residual = pl.pallas_call(
         functools.partial(whole_kernel, orients, coefs, own_coefs),
@@ -361,9 +401,7 @@
         scratch_shapes=[
             pltpu.VMEM((4, tables, grid_size), WIDE),
             pltpu.VMEM((2, images, grid_size, grid_size), WIDE),
-            table,
-            table,
-            table,
+            *[table] * 6,
             pltpu.VMEM((images, grid_size, grid_size), WIDE),
             pltpu.VMEM((coefs, tables, padded, segs), WIDE),
             pltpu.VMEM((planes, padded, grid_size), WIDE),

time: 65.9 us -> 44 us (0.67)
  Pallas kernels: 59 us -> 37.1 us
    pallas_call x1, Pallas kernels: 59 us -> 37.1 us  [body(): pl.pallas_call(functools.partial(whole_kernel, orients, coefs, own_coefs)...]
where the time goes in v3:
time: 44 us; the launch traced here: 43.8 us
  Pallas kernels  37.1 us (84%)
  local copies, waits for them, and re-layouts  4.71 us (11%)
  between operations  1.35 us (3%)
  other arithmetic  0.63 us (1%)
    pallas_call x1, Pallas kernels, body(): pl.pallas_call(functools.partial(whole_kernel, orients, coefs, own_coefs)...  37.1 us
    unnamed x11, local copies, waits for them, and re-layouts  4.63 us

profile of v3, /device:TPU:0, one launch (start us, length us, event | category | flops | bytes accessed | tf_op | source)
XLA Modules:
  0.0 43.8 jit_solution(4722720754733898122)
XLA Ops:
  1.3 0.0 copy-start.3
  1.3 0.6 %copy-done.3 = f32[16]{0:T(128)S(1)} copy-done((f32[16]{0:T(128)S(1)}, f32[16]{0:T(128)}, u32[]{:S(2)}) %copy-start.3) | copy-done | bytes 88
  2.0 0.1 broadcast_in_dim.35.angle_ref
  2.0 0.0 copy-start.1
  2.0 0.9 %copy.10 = f32[16,64,6]{1,2,0:T(8,128)S(1)} copy(f32[16,64,6]{1,0,2:T(8,128)} %param.8) | data formatting | bytes 49152 | tf_op args[2]
  2.9 0.6 %multiply_convert_fusion = (bf16[128,128]{1,0:T(8,128)(2,1)S(1)}, bf16[128,128]{1,0:T(8,128)(2,1)S(1)}, bf16[128,128]{1,0:T(8,128)(2,1)S(1)}, bf16[128,128]{1,0:T(8,128)(2,1)S(1)}) fusion(f32[128]{0:T(128)S(1)} %or_select_fusion, s32[128]{0:T(128)S(1)} %compare_select_fusion, pred[128]{0:T(512)(128)(4,1)S(1)} %iota_compare_fusion), kind=kLoop, calls=%fused_computation.13 | loop fusion | flops 589824 | bytes 132224 | tf_op jit(solution)/shard_map/convert_element_type | solution.py:26
  3.5 0.0 copy-start.2
  3.5 0.0 copy-done.1
  3.5 0.6 %copy-done.2 = s32[1,64]{1,0:T(1,128)S(1)} copy-done((s32[1,64]{1,0:T(1,128)S(1)}, s32[1,64]{1,0:T(1,128)}, u32[]{:S(2)}) %copy-start.2) | copy-done | bytes 280
  4.2 0.0 copy-start
  4.2 1.0 %copy-done = f32[1,16,64,128]{3,2,1,0:T(8,128)S(1)} copy-done((f32[1,16,64,128]{3,2,1,0:T(8,128)S(1)}, f32[1,16,64,128]{3,2,1,0:T(8,128)}, u32[]{:S(2)}) %copy-start) | copy-done | bytes 524312
  5.2 37.1 %shard_map.77 = (f32[6,128,128]{2,1,0:T(8,128)S(1)}, f32[16,32,128]{2,1,0:T(8,128)S(1)}) custom-call(bf16[6,128,128]{2,1,0:T(8,128)(2,1)S(1)} %bitcast.10, f32[16,64,128]{2,1,0:T(8,128)S(1)} %bitcast.7, f32[16,8,64]{2,1,0:T(8,128)S(1)} %pad.4.basis_ref, f32[16,128]{1,0:T(8,128)S(1)} %broadcast_in_dim.35.angle_ref, s32[1]{0:T(128)S(6)} %copy.13.index_ref, ...), custom_call_target="tpu_custom_call" | custom-call | tf_op jit(solution)/shard_map/pallas_call | solution.py:393
  42.4 0.7 %copy.14 = f32[1,6,128,128]{3,2,1,0:T(8,128)} copy(f32[1,6,128,128]{3,2,1,0:T(8,128)S(1)} %bitcast.8) | data formatting | bytes 786432
  43.1 0.7 %copy.15 = f32[1,16,32,128]{3,2,1,0:T(8,128)} copy(f32[1,16,32,128]{3,2,1,0:T(8,128)S(1)} %bitcast.9) | data formatting | bytes 524288
  (4 shorter events, 0.0 us)
Async XLA Ops:
  1.3 0.7 %copy-start.3 = (f32[16]{0:T(128)S(1)}, f32[16]{0:T(128)}, u32[]{:S(2)}) copy-start(f32[16]{0:T(128)} %param.9) | copy-start | bytes 196
  2.0 1.5 %copy-start.1 = (bf16[1,6,128,128]{3,2,1,0:T(8,128)(2,1)S(1)}, bf16[1,6,128,128]{3,2,1,0:T(8,128)(2,1)}, u32[]{:S(2)}) copy-start(bf16[1,6,128,128]{3,2,1,0:T(8,128)(2,1)} %param.6) | copy-start | bytes 589828
  3.5 0.7 %copy-start.2 = (s32[1,64]{1,0:T(1,128)S(1)}, s32[1,64]{1,0:T(1,128)}, u32[]{:S(2)}) copy-start(s32[1,64]{1,0:T(1,128)} %map_ref.1) | copy-start | bytes 772
  4.2 1.0 %copy-start = (f32[1,16,64,128]{3,2,1,0:T(8,128)S(1)}, f32[1,16,64,128]{3,2,1,0:T(8,128)}, u32[]{:S(2)}) copy-start(f32[1,16,64,128]{3,2,1,0:T(8,128)} %param.7) | copy-start | bytes 1572868

commit v4 on v3

--- a/solution.py
+++ b/solution.py
@@ -187,7 +187,7 @@
     orients, coefs, own_coefs,
     volume_ref, data_ref, basis_ref, angle_ref, index_ref, map_ref, ana_ref, ana_t_ref, syn_ref, syn_t_ref,
     grad_ref, resid_ref,
-    unit_ref, spec_ref, row_a, col_a, mix_a, row_b, col_b, mix_b, total_ref,
+    unit_ref, spec_ref, sides, total_ref,
     basis_all, pull_out, pull_in, prof_all, back_out, back_in,
     basis_send, basis_recv, pull_send, pull_recv, prof_send, prof_recv, back_send, back_recv,
 ):
@@ -276,19 +276,19 @@
 
     filler = jnp.zeros((padded - images, grid_size), WIDE)
 
-    sides = ((row_a, col_a, mix_a), (row_b, col_b, mix_b))
-    pairs = tables // 2
+    width = len(sides)
+    pairs = tables // width
 
     def project(slot, carry):
         for side, refs in enumerate(sides):
-            build_tables(2 * slot + side, grid_size, unit_ref, *refs, slot, syn_ref[...])
+            build_tables(width * slot + side, grid_size, unit_ref, *refs, slot, syn_ref[...])
         waves = (ana_ref[...], ana_t_ref[...], syn_ref[...])
         profiles = forward_pair(slot, images, grid_size, spec_ref, sides, waves)
         for side, rows in enumerate(profiles):
-            prof_all[2 * slot + side, mine] = jnp.concatenate([rows, filler], axis=0)
-        for side in range(2):
+            prof_all[width * slot + side, mine] = jnp.concatenate([rows, filler], axis=0)
+        for side in range(width):
             for step in range(1, coefs):
-                prof_copy(step, 2 * slot + side).start()
+                prof_copy(step, width * slot + side).start()
         return carry
 
     lax.fori_loop(0, pairs, project, 0)
@@ -298,15 +298,15 @@
     over_steps(lambda step: pull_copy(step).wait())
 
     def arrived(slot, carry):
-        for side in range(2):
+        for side in range(width):
             for step in range(1, coefs):
-                prof_copy(step, 2 * slot + side).wait()
+                prof_copy(step, width * slot + side).wait()
         return carry
 
     def contract(slot):
         found = []
-        for side in range(2):
-            which = 2 * slot + side
+        for side in range(width):
+            which = width * slot + side
             rows = jnp.zeros((padded, grid_size), WIDE)
             for orient in range(orients):
                 block = pull_in[orient]
@@ -388,7 +388,8 @@
     basis = jnp.pad(basis_table.transpose(0, 2, 1), ((0, 0), (0, padded - own_coefs), (0, 0)))
     vmem = pl.BlockSpec(memory_space=pltpu.VMEM)
     smem = pl.BlockSpec(memory_space=pltpu.SMEM)
-    table = pltpu.VMEM((tables // 2, 2, grid_size, grid_size), WIDE)
+    width = math.gcd(tables, 4)
+    table = pltpu.VMEM((tables // width, 2, grid_size, grid_size), WIDE)
     dma = pltpu.SemaphoreType.DMA
     gradient, residual = pl.pallas_call(
         functools.partial(whole_kernel, orients, coefs, own_coefs),
@@ -401,7 +402,7 @@
         scratch_shapes=[
             pltpu.VMEM((4, tables, grid_size), WIDE),
             pltpu.VMEM((2, images, grid_size, grid_size), WIDE),
-            *[table] * 6,
+            tuple((table, table, table) for _ in range(width)),
             pltpu.VMEM((images, grid_size, grid_size), WIDE),
             pltpu.VMEM((coefs, tables, padded, segs), WIDE),
             pltpu.VMEM((planes, padded, grid_size), WIDE),

time: 44 us -> 35.4 us (0.80)
  Pallas kernels: 37.1 us -> 28.5 us
    pallas_call x1, Pallas kernels: 37.1 us -> 28.5 us  [body(): pl.pallas_call(functools.partial(whole_kernel, orients, coefs, own_coefs)...]
where the time goes in v4:
time: 35.4 us; the launch traced here: 35.2 us
  Pallas kernels  28.5 us (81%)
  local copies, waits for them, and re-layouts  4.71 us (13%)
  between operations  1.35 us (4%)
  other arithmetic  0.63 us (2%)
    pallas_call x1, Pallas kernels, body(): pl.pallas_call(functools.partial(whole_kernel, orients, coefs, own_coefs)...  28.5 us
    unnamed x11, local copies, waits for them, and re-layouts  4.63 us

profile of v4, /device:TPU:0, one launch (start us, length us, event | category | flops | bytes accessed | tf_op | source)
XLA Modules:
  0.0 35.2 jit_solution(2288353157784548852)
XLA Ops:
  1.3 0.0 copy-start.3
  1.3 0.6 %copy-done.3 = f32[16]{0:T(128)S(1)} copy-done((f32[16]{0:T(128)S(1)}, f32[16]{0:T(128)}, u32[]{:S(2)}) %copy-start.3) | copy-done | bytes 88
  2.0 0.1 broadcast_in_dim.35.angle_ref
  2.0 0.0 copy-start.1
  2.0 0.9 %copy.10 = f32[16,64,6]{1,2,0:T(8,128)S(1)} copy(f32[16,64,6]{1,0,2:T(8,128)} %param.8) | data formatting | bytes 49152 | tf_op args[2]
  2.9 0.6 %multiply_convert_fusion = (bf16[128,128]{1,0:T(8,128)(2,1)S(1)}, bf16[128,128]{1,0:T(8,128)(2,1)S(1)}, bf16[128,128]{1,0:T(8,128)(2,1)S(1)}, bf16[128,128]{1,0:T(8,128)(2,1)S(1)}) fusion(f32[128]{0:T(128)S(1)} %or_select_fusion, s32[128]{0:T(128)S(1)} %compare_select_fusion, pred[128]{0:T(512)(128)(4,1)S(1)} %iota_compare_fusion), kind=kLoop, calls=%fused_computation.13 | loop fusion | flops 589824 | bytes 132224 | tf_op jit(solution)/shard_map/convert_element_type | solution.py:26
  3.5 0.0 copy-start.2
  3.5 0.0 copy-done.1
  3.5 0.6 %copy-done.2 = s32[1,64]{1,0:T(1,128)S(1)} copy-done((s32[1,64]{1,0:T(1,128)S(1)}, s32[1,64]{1,0:T(1,128)}, u32[]{:S(2)}) %copy-start.2) | copy-done | bytes 280
  4.2 0.0 copy-start
  4.2 1.0 %copy-done = f32[1,16,64,128]{3,2,1,0:T(8,128)S(1)} copy-done((f32[1,16,64,128]{3,2,1,0:T(8,128)S(1)}, f32[1,16,64,128]{3,2,1,0:T(8,128)}, u32[]{:S(2)}) %copy-start) | copy-done | bytes 524312
  5.2 28.5 %shard_map.77 = (f32[6,128,128]{2,1,0:T(8,128)S(1)}, f32[16,32,128]{2,1,0:T(8,128)S(1)}) custom-call(bf16[6,128,128]{2,1,0:T(8,128)(2,1)S(1)} %bitcast.10, f32[16,64,128]{2,1,0:T(8,128)S(1)} %bitcast.7, f32[16,8,64]{2,1,0:T(8,128)S(1)} %pad.4.basis_ref, f32[16,128]{1,0:T(8,128)S(1)} %broadcast_in_dim.35.angle_ref, s32[1]{0:T(128)S(6)} %copy.13.index_ref, ...), custom_call_target="tpu_custom_call" | custom-call | tf_op jit(solution)/shard_map/pallas_call | solution.py:394
  33.7 0.7 %copy.14 = f32[1,6,128,128]{3,2,1,0:T(8,128)} copy(f32[1,6,128,128]{3,2,1,0:T(8,128)S(1)} %bitcast.8) | data formatting | bytes 786432
  34.5 0.7 %copy.15 = f32[1,16,32,128]{3,2,1,0:T(8,128)} copy(f32[1,16,32,128]{3,2,1,0:T(8,128)S(1)} %bitcast.9) | data formatting | bytes 524288
  (4 shorter events, 0.0 us)
Async XLA Ops:
  1.3 0.7 %copy-start.3 = (f32[16]{0:T(128)S(1)}, f32[16]{0:T(128)}, u32[]{:S(2)}) copy-start(f32[16]{0:T(128)} %param.9) | copy-start | bytes 196
  2.0 1.5 %copy-start.1 = (bf16[1,6,128,128]{3,2,1,0:T(8,128)(2,1)S(1)}, bf16[1,6,128,128]{3,2,1,0:T(8,128)(2,1)}, u32[]{:S(2)}) copy-start(bf16[1,6,128,128]{3,2,1,0:T(8,128)(2,1)} %param.6) | copy-start | bytes 589828
  3.5 0.7 %copy-start.2 = (s32[1,64]{1,0:T(1,128)S(1)}, s32[1,64]{1,0:T(1,128)}, u32[]{:S(2)}) copy-start(s32[1,64]{1,0:T(1,128)} %map_ref.1) | copy-start | bytes 772
  4.2 1.0 %copy-start = (f32[1,16,64,128]{3,2,1,0:T(8,128)S(1)}, f32[1,16,64,128]{3,2,1,0:T(8,128)}, u32[]{:S(2)}) copy-start(f32[1,16,64,128]{3,2,1,0:T(8,128)} %param.7) | copy-start | bytes 1572868

commit v5 on v4

--- a/solution.py
+++ b/solution.py
@@ -174,7 +174,7 @@
 
 
 MESH = pl.DeviceIdType.MESH
-LIMIT = 48 << 20
+LIMIT = 63 << 20
 
 
 def exact(left, right, contract=((1,), (0,))):
@@ -185,8 +185,8 @@
 
 def whole_kernel(
     orients, coefs, own_coefs,
-    volume_ref, data_ref, basis_ref, angle_ref, index_ref, map_ref, ana_ref, ana_t_ref, syn_ref, syn_t_ref,
-    grad_ref, resid_ref,
+    volume_hbm, data_hbm, table_hbm, angle_ref, index_ref, map_hbm, ana_ref, ana_t_ref, syn_ref, syn_t_ref,
+    grad_ref, resid_ref, volume_ref, table_ref, data_ref, map_ref, basis_ref, fetch_sem,
     unit_ref, spec_ref, sides, total_ref,
     basis_all, pull_out, pull_in, prof_all, back_out, back_in,
     basis_send, basis_recv, pull_send, pull_recv, prof_send, prof_recv, back_send, back_recv,
@@ -194,6 +194,14 @@
     me, mine = lax.axis_index("orient"), lax.axis_index("coef")
     images, grid_size = volume_ref.shape[0], volume_ref.shape[-1]
     tables, padded, segs = basis_ref.shape
+    data_copy = pltpu.make_async_copy(data_hbm, data_ref, fetch_sem.at[0])
+    map_copy = pltpu.make_async_copy(map_hbm, map_ref, fetch_sem.at[1])
+    table_copy = pltpu.make_async_copy(table_hbm, table_ref, fetch_sem.at[2])
+    volume_copy = pltpu.make_async_copy(volume_hbm, volume_ref, fetch_sem.at[3])
+    table_copy.start()
+    map_copy.start()
+    volume_copy.start()
+    data_copy.start()
     planes = data_ref.shape[0]
     share = resid_ref.shape[1]
 
@@ -249,9 +257,19 @@
             barrier, inc=1, device_id=(me, lax.rem(mine + step, coefs)), device_id_type=MESH
         )
 
-    unit_waves(angle_ref[...], grid_size, unit_ref)
+    row_ids = lax.broadcasted_iota(jnp.int32, (tables, grid_size), 0)
+    angles = jnp.zeros((tables, grid_size), WIDE)
+    for which in range(tables):
+        angles = jnp.where(row_ids == which, angle_ref[which], angles)
+    unit_waves(angles, grid_size, unit_ref)
+    basis_ref[...] = jnp.zeros_like(basis_ref)
+    table_copy.wait()
+    for coef in range(own_coefs):
+        basis_ref[:, coef, :] = table_ref[coef]
+    volume_copy.wait()
     volume_spectra(volume_ref, ana_t_ref[...], spec_ref, images, grid_size)
     total_ref[...] = jnp.zeros_like(total_ref)
+    map_copy.wait()
     map_row = map_ref[...]
     chosen = (lax.broadcasted_iota(jnp.int32, (segs, segs), 0) == map_row).astype(WIDE)
     index = index_ref[0]
@@ -259,6 +277,7 @@
     tag_row = lax.broadcasted_iota(jnp.int32, (padded, grid_size), 0) == own_coefs
     tag = index.astype(WIDE)
 
+    data_copy.wait()
     mix_parts = jnp.concatenate(split(own_mix_t), axis=0)
 
     def pull_one(plane, carry):
@@ -384,8 +403,7 @@
     share = segs // coefs
     padded = (own_coefs + 8) // 8 * 8
     analysis, synthesis = dft_tables(grid_size)
-    angles = jnp.broadcast_to(angle_table[:, None], (tables, grid_size))
-    basis = jnp.pad(basis_table.transpose(0, 2, 1), ((0, 0), (0, padded - own_coefs), (0, 0)))
+    far = pl.BlockSpec(memory_space=pltpu.HBM)
     vmem = pl.BlockSpec(memory_space=pltpu.VMEM)
     smem = pl.BlockSpec(memory_space=pltpu.SMEM)
     width = math.gcd(tables, 4)
@@ -397,9 +415,15 @@
             jax.ShapeDtypeStruct((images, grid_size, grid_size), WIDE),
             jax.ShapeDtypeStruct((planes, share, grid_size), WIDE),
         ),
-        in_specs=[vmem] * 4 + [smem] + [vmem] * 5,
+        in_specs=[far, far, far, smem, smem, far] + [vmem] * 4,
         out_specs=(vmem, vmem),
         scratch_shapes=[
+            pltpu.VMEM((images, grid_size, grid_size), NARROW),
+            pltpu.VMEM((own_coefs, tables, segs), WIDE),
+            pltpu.VMEM((planes, segs, grid_size), WIDE),
+            pltpu.VMEM((1, segs), jnp.int32),
+            pltpu.VMEM((tables, padded, segs), WIDE),
+            dma((4,)),
             pltpu.VMEM((4, tables, grid_size), WIDE),
             pltpu.VMEM((2, images, grid_size, grid_size), WIDE),
             tuple((table, table, table) for _ in range(width)),
@@ -425,8 +449,8 @@
     )(
         volume.reshape(images, grid_size, grid_size),
         measured[0],
-        basis,
-        angles,
+        basis_table.transpose(2, 0, 1),
+        angle_table,
         angle_index,
         sector_map,
         analysis,

time: 35.4 us -> 35.3 us (level)
  local copies, waits for them, and re-layouts: 4.71 us -> 2.52 us
  Pallas kernels: 28.5 us -> 29.9 us
  other arithmetic: 0.63 us -> 1.26 us
    unnamed x11 -> x4, local copies, waits for them, and re-layouts: 4.63 us -> 2.52 us
    pallas_call x1, Pallas kernels: 28.5 us -> 29.9 us  [body(): pl.pallas_call(functools.partial(whole_kernel, orients, coefs, own_coefs)...]
    convert_element_type x1, other arithmetic: 0.61 us -> 1.25 us  [dft_tables(): (base_wave * weights[:, None]).astype(jnp.bfloat16)]
where the time goes in v5:
time: 35.3 us; the launch traced here: 35 us
  Pallas kernels  29.9 us (85%)
  local copies, waits for them, and re-layouts  2.52 us (7%)
  between operations  1.31 us (4%)
  other arithmetic  1.26 us (4%)
    pallas_call x1, Pallas kernels, body(): pl.pallas_call(functools.partial(whole_kernel, orients, coefs, own_coefs)...  29.9 us
    unnamed x4, local copies, waits for them, and re-layouts  2.52 us
    convert_element_type x1, other arithmetic, dft_tables(): (base_wave * weights[:, None]).astype(jnp.bfloat16)  1.25 us

profile of v5, /device:TPU:0, one launch (start us, length us, event | category | flops | bytes accessed | tf_op | source)
XLA Modules:
  0.0 35.0 jit_solution(13042034455245041740)
XLA Ops:
  1.3 1.2 %multiply_convert_fusion = (bf16[128,128]{1,0:T(8,128)(2,1)}, bf16[128,128]{1,0:T(8,128)(2,1)}, bf16[128,128]{1,0:T(8,128)(2,1)}, bf16[128,128]{1,0:T(8,128)(2,1)}) fusion(f32[128]{0:T(128)S(1)} %or_select_fusion, s32[128]{0:T(128)S(1)} %compare_select_fusion, pred[128]{0:T(512)(128)(4,1)S(1)} %iota_compare_fusion), kind=kLoop, calls=%fused_computation.12 | loop fusion | flops 589824 | bytes 132224 | tf_op jit(solution)/shard_map/convert_element_type | solution.py:26
  2.6 29.9 %shard_map.77 = (f32[6,128,128]{2,1,0:T(8,128)}, f32[16,32,128]{2,1,0:T(8,128)}) custom-call(bf16[6,128,128]{2,1,0:T(8,128)(2,1)} %bitcast.8, f32[16,64,128]{2,1,0:T(8,128)} %bitcast.5, f32[6,16,64]{2,1,0:T(8,128)} %bitcast.9, f32[16]{0:T(128)} %angle_ref.1, s32[1]{0:T(128)S(6)} %copy.10.index_ref, s32[1,64]{1,0:T(1,128)} %map_hbm.1, ...), custom_call_target="tpu_custom_call" | custom-call | tf_op jit(solution)/shard_map/pallas_call | solution.py:412
  32.5 0.0 copy-start
  32.5 1.8 %copy.11 = f32[1,6,128,128]{3,2,1,0:T(8,128)} copy(f32[1,6,128,128]{3,2,1,0:T(8,128)} %bitcast.6) | data formatting | bytes 786432
  34.3 0.0 copy-done
  34.3 0.7 %copy.12 = f32[1,16,32,128]{3,2,1,0:T(8,128)} copy(f32[1,16,32,128]{3,2,1,0:T(8,128)S(1)} %bitcast.7) | data formatting | bytes 524288
  (3 shorter events, 0.0 us)
Async XLA Ops:
  32.5 1.8 %copy-start = (f32[16,32,128]{2,1,0:T(8,128)S(1)}, f32[16,32,128]{2,1,0:T(8,128)}, u32[]{:S(2)}) copy-start(f32[16,32,128]{2,1,0:T(8,128)} %get-tuple-element.5) | copy-start | bytes 786436

commit v6 on v5

--- a/solution.py
+++ b/solution.py
@@ -406,7 +406,7 @@
     far = pl.BlockSpec(memory_space=pltpu.HBM)
     vmem = pl.BlockSpec(memory_space=pltpu.VMEM)
     smem = pl.BlockSpec(memory_space=pltpu.SMEM)
-    width = math.gcd(tables, 4)
+    width = math.gcd(tables, 8)
     table = pltpu.VMEM((tables // width, 2, grid_size, grid_size), WIDE)
     dma = pltpu.SemaphoreType.DMA
     gradient, residual = pl.pallas_call(

time: 35.3 us -> 30.7 us (0.87)
  Pallas kernels: 29.9 us -> 25.4 us
    pallas_call x1, Pallas kernels: 29.9 us -> 25.4 us  [body(): pl.pallas_call(functools.partial(whole_kernel, orients, coefs, own_coefs)...]
where the time goes in v6:
time: 30.7 us; the launch traced here: 30.4 us
  Pallas kernels  25.4 us (83%)
  local copies, waits for them, and re-layouts  2.52 us (8%)
  between operations  1.31 us (4%)
  other arithmetic  1.26 us (4%)
    pallas_call x1, Pallas kernels, body(): pl.pallas_call(functools.partial(whole_kernel, orients, coefs, own_coefs)...  25.4 us
    unnamed x4, local copies, waits for them, and re-layouts  2.52 us
    convert_element_type x1, other arithmetic, dft_tables(): (base_wave * weights[:, None]).astype(jnp.bfloat16)  1.25 us

profile of v6, /device:TPU:0, one launch (start us, length us, event | category | flops | bytes accessed | tf_op | source)
XLA Modules:
  0.0 30.4 jit_solution(8966345655760355643)
XLA Ops:
  1.3 1.2 %multiply_convert_fusion = (bf16[128,128]{1,0:T(8,128)(2,1)}, bf16[128,128]{1,0:T(8,128)(2,1)}, bf16[128,128]{1,0:T(8,128)(2,1)}, bf16[128,128]{1,0:T(8,128)(2,1)}) fusion(f32[128]{0:T(128)S(1)} %or_select_fusion, s32[128]{0:T(128)S(1)} %compare_select_fusion, pred[128]{0:T(512)(128)(4,1)S(1)} %iota_compare_fusion), kind=kLoop, calls=%fused_computation.12 | loop fusion | flops 589824 | bytes 132224 | tf_op jit(solution)/shard_map/convert_element_type | solution.py:26
  2.6 25.4 %shard_map.77 = (f32[6,128,128]{2,1,0:T(8,128)}, f32[16,32,128]{2,1,0:T(8,128)}) custom-call(bf16[6,128,128]{2,1,0:T(8,128)(2,1)} %bitcast.8, f32[16,64,128]{2,1,0:T(8,128)} %bitcast.5, f32[6,16,64]{2,1,0:T(8,128)} %bitcast.9, f32[16]{0:T(128)} %angle_ref.1, s32[1]{0:T(128)S(6)} %copy.10.index_ref, s32[1,64]{1,0:T(1,128)} %map_hbm.1, ...), custom_call_target="tpu_custom_call" | custom-call | tf_op jit(solution)/shard_map/pallas_call | solution.py:412
  27.9 0.0 copy-start
  27.9 1.8 %copy.11 = f32[1,6,128,128]{3,2,1,0:T(8,128)} copy(f32[1,6,128,128]{3,2,1,0:T(8,128)} %bitcast.6) | data formatting | bytes 786432
  29.7 0.0 copy-done
  29.7 0.7 %copy.12 = f32[1,16,32,128]{3,2,1,0:T(8,128)} copy(f32[1,16,32,128]{3,2,1,0:T(8,128)S(1)} %bitcast.7) | data formatting | bytes 524288
  (3 shorter events, 0.0 us)
Async XLA Ops:
  27.9 1.8 %copy-start = (f32[16,32,128]{2,1,0:T(8,128)S(1)}, f32[16,32,128]{2,1,0:T(8,128)}, u32[]{:S(2)}) copy-start(f32[16,32,128]{2,1,0:T(8,128)} %get-tuple-element.5) | copy-start | bytes 786436

commit v7 on v6

--- a/solution.py
+++ b/solution.py
@@ -338,10 +338,13 @@
             found.append((spectra, pltpu.roll(spectra, grid_size // 2, 1)))
         return tuple(found)
 
+    def last_back(slot, spectra):
+        waves = (ana_ref[...], ana_t_ref[...], syn_t_ref[...])
+        backward_pair(slot, spectra, images, grid_size, total_ref, sides, waves)
+
     def spread_back(slot, spectra):
-        waves = (ana_ref[...], ana_t_ref[...], syn_t_ref[...])
-        following = contract(jnp.minimum(slot + 1, pairs - 1))
-        backward_pair(slot, spectra, images, grid_size, total_ref, sides, waves)
+        following = contract(slot + 1)
+        last_back(slot, spectra)
         return following
 
     def first_part(slot, spectra):
@@ -367,9 +370,11 @@
     lax.fori_loop(0, orients, return_one, 0)
     back_in[me] = back_out[me]
     over_steps(lambda step: back_copy(step).start())
-    lax.fori_loop(early, pairs, spread_back, spectra)
+    if early < pairs - 1:
+        spectra = lax.fori_loop(early, pairs - 1, spread_back, spectra)
+    last_back(pairs - 1, spectra)
     for image in range(images):
-        grad_ref[image] = mul(total_ref[image].astype(NARROW), ana_ref[...])
+        grad_ref[image] = total_ref[image].astype(NARROW)
 
     row_ids = lax.broadcasted_iota(jnp.int32, (share, segs), 0) + mine * share
     lane_ids = lax.broadcasted_iota(jnp.int32, (share, segs), 1)
@@ -403,16 +408,19 @@
     share = segs // coefs
     padded = (own_coefs + 8) // 8 * 8
     analysis, synthesis = dft_tables(grid_size)
+    analysis, analysis_t, synthesis, synthesis_t = lax.optimization_barrier(
+        (analysis, analysis.T, synthesis, synthesis.T)
+    )
     far = pl.BlockSpec(memory_space=pltpu.HBM)
     vmem = pl.BlockSpec(memory_space=pltpu.VMEM)
     smem = pl.BlockSpec(memory_space=pltpu.SMEM)
     width = math.gcd(tables, 8)
     table = pltpu.VMEM((tables // width, 2, grid_size, grid_size), WIDE)
     dma = pltpu.SemaphoreType.DMA
-    gradient, residual = pl.pallas_call(
+    summed, residual = pl.pallas_call(
         functools.partial(whole_kernel, orients, coefs, own_coefs),
         out_shape=(
-            jax.ShapeDtypeStruct((images, grid_size, grid_size), WIDE),
+            jax.ShapeDtypeStruct((images, grid_size, grid_size), NARROW),
             jax.ShapeDtypeStruct((planes, share, grid_size), WIDE),
         ),
         in_specs=[far, far, far, smem, smem, far] + [vmem] * 4,
@@ -454,10 +462,11 @@
         angle_index,
         sector_map,
         analysis,
-        analysis.T,
+        analysis_t,
         synthesis,
-        synthesis.T,
-    )
+        synthesis_t,
+    )
+    gradient = jnp.einsum("cyr,rx->cyx", summed, analysis, preferred_element_type=WIDE)
     return (gradient.reshape(volume.shape), residual[None])
 
 

time: 30.7 us -> 30.8 us (level)
  matrix products: 0 us -> 1.9 us
  local copies, waits for them, and re-layouts: 2.52 us -> 0.71 us
    dot_general x0 -> x1, matrix products: none -> 1.9 us  [body(): jnp.einsum('cyr,rx->cyx', summed, analysis, preferred_element_type=WIDE)]
    unnamed x4 -> x5, local copies, waits for them, and re-layouts: 2.52 us -> 0.71 us
where the time goes in v7:
time: 30.8 us; the launch traced here: 30.6 us
  Pallas kernels  25.4 us (82%)
  matrix products  1.9 us (6%)
  between operations  1.32 us (4%)
  other arithmetic  1.26 us (4%)
  local copies, waits for them, and re-layouts  0.71 us (2%)
    pallas_call x1, Pallas kernels, body(): pl.pallas_call(functools.partial(whole_kernel, orients, coefs, own_coefs)...  25.4 us
    dot_general x1, matrix products, body(): jnp.einsum('cyr,rx->cyx', summed, analysis, preferred_element_type=WIDE)  1.9 us
    convert_element_type x1, other arithmetic, dft_tables(): (base_wave * weights[:, None]).astype(jnp.bfloat16)  1.25 us
    unnamed x5, local copies, waits for them, and re-layouts  0.71 us

profile of v7, /device:TPU:0, one launch (start us, length us, event | category | flops | bytes accessed | tf_op | source)
XLA Modules:
  0.0 30.6 jit_solution(387259074655716180)
XLA Ops:
  1.3 1.2 %multiply_convert_fusion = (bf16[128,128]{1,0:T(8,128)(2,1)}, bf16[128,128]{1,0:T(8,128)(2,1)}, bf16[128,128]{1,0:T(8,128)(2,1)}, bf16[128,128]{1,0:T(8,128)(2,1)}) fusion(f32[128]{0:T(128)S(1)} %or_select_fusion, s32[128]{0:T(128)S(1)} %compare_select_fusion, pred[128]{0:T(512)(128)(4,1)S(1)} %iota_compare_fusion), kind=kLoop, calls=%fused_computation.13 | loop fusion | flops 589824 | bytes 132224 | tf_op jit(solution)/shard_map/convert_element_type | solution.py:26
  2.6 0.0 copy-start
  2.6 25.4 %shard_map.77 = (bf16[6,128,128]{2,1,0:T(8,128)(2,1)}, f32[16,32,128]{2,1,0:T(8,128)}) custom-call(bf16[6,128,128]{2,1,0:T(8,128)(2,1)} %bitcast.12, f32[16,64,128]{2,1,0:T(8,128)} %bitcast.10, f32[6,16,64]{2,1,0:T(8,128)} %bitcast.13, f32[16]{0:T(128)} %angle_ref.1, s32[1]{0:T(128)S(6)} %copy.9.index_ref, s32[1,64]{1,0:T(1,128)} %map_hbm.1, ...), custom_call_target="tpu_custom_call" | custom-call | tf_op jit(solution)/shard_map/pallas_call | solution.py:420
  27.9 0.0 copy-done
  27.9 0.0 copy-start.1
  28.0 1.9 %convolution_bitcast_fusion = f32[1,6,128,128]{3,2,1,0:T(8,128)} fusion(bf16[6,128,128]{2,1,0:T(8,128)(2,1)} %get-tuple-element.12, bf16[128,128]{1,0:T(8,128)(2,1)S(1)} %copy-done), kind=kOutput, calls=%fused_computation | convolution fusion | flops 25165824 | bytes 622592 | tf_op jit(solution)/shard_map/cyr,rx->cyx/dot_general | solution.py:469
  29.9 0.0 copy-done.1
  29.9 0.7 %copy.10 = f32[1,16,32,128]{3,2,1,0:T(8,128)} copy(f32[1,16,32,128]{3,2,1,0:T(8,128)S(1)} %bitcast.11) | data formatting | bytes 524288
  (3 shorter events, 0.0 us)
Async XLA Ops:
  2.6 25.4 %copy-start = (bf16[128,128]{1,0:T(8,128)(2,1)S(1)}, bf16[128,128]{1,0:T(8,128)(2,1)}, u32[]{:S(2)}) copy-start(bf16[128,128]{1,0:T(8,128)(2,1)} %get-tuple-element.8.ana_ref) | copy-start | bytes 98308
  27.9 1.9 %copy-start.1 = (f32[16,32,128]{2,1,0:T(8,128)S(1)}, f32[16,32,128]{2,1,0:T(8,128)}, u32[]{:S(2)}) copy-start(f32[16,32,128]{2,1,0:T(8,128)} %get-tuple-element.13) | copy-start | bytes 786436
